TPU v7x, 32 devices: a whole 2x2x4 slice. The times are simulated.
32 devices in a mesh: ctx: 8 (over z, y), head: 4 (over x, core).
Axes of the slice: x: 2, y: 2, z: 4, core: 2. Of those that a mesh axis runs over, the one named last changes fastest.
Arguments:
- queries: bfloat16 [4096, 5120], P('ctx', 'head'), may hold values from -34 to 34
- key_rows: bfloat16 [4096, 5120], P('ctx', 'head'), may hold values from -8 to 8
- value_rows: bfloat16 [4096, 5120], P('ctx', 'head'), may hold values from -23 to 23
- learning_rates: float32 [8, 4096], P('head', 'ctx'), may hold values from 0.02 to 1
- fast_gate: bfloat16 [8, 640, 640], P('head'), may hold values from -0.25 to 0.25
- fast_lift: bfloat16 [8, 640, 640], P('head'), may hold values from -0.25 to 0.25
- fast_down: bfloat16 [8, 640, 640], P('head'), may hold values from -0.25 to 0.25
- output_gain: float32 [5120], P('head'), may hold values from 0.25 to 1.75
- output_weight: bfloat16 [5120, 5120], P(None, 'head'), may hold values from -0.078125 to 0.078125
Outputs:
- layer_output: bfloat16 [4096, 5120], P('ctx', 'head')
All inputs are finite; a program needn't handle non-finite values.
Results may differ from a plain program's by a relative error of at most 0.025.
Values may be sent and summed in bfloat16 or wider, within the bound.
No kernel may reach another device: no remote copies, remote signals or barrier semaphores. Data moves between devices by JAX's collectives and lax.ppermute only.
A program may use at most 128 MiB of HBM per device.

v0:
```python
import functools
import math

import jax
import jax.numpy as jnp
from jax import lax
from jax.experimental import pallas as pl
from jax.experimental.pallas import tpu as pltpu
from jax.sharding import PartitionSpec as P

ATT_HD = 128
WINDOW = 512
NS_ITERS = 3
PIECES = 2
VMEM_BYTES = 24 * 1024 * 1024
PROJECT_BYTES = 58 * 1024 * 1024

quintic_first = 3.4445
quintic_second = -4.775
quintic_third = 2.0315

f32 = jnp.float32
bf16 = jnp.bfloat16


def mm(a, b, dims=((1,), (0,))):
    return lax.dot_general(a, b, (dims, ((), ())), preferred_element_type=f32)


def after(value, *earlier):
    return lax.optimization_barrier((value, *earlier))[0]


def pick(blocks, which):
    out = blocks[0]
    for number in range(1, len(blocks)):
        out = jnp.where(which == number, blocks[number], out)
    return out


def tree_low(low, high):
    levels, step = [], 1
    while step < high - low:
        levels.append(
            [(i + step, i) for i in range(low, high, 2 * step) if i + step < high]
        )
        step *= 2
    return levels


def tree_high(low, high):
    return [
        [(low + high - 1 - a, low + high - 1 - b) for a, b in level]
        for level in tree_low(low, high)
    ]


def tree_ends(count):
    low = tree_low(0, count // 2)
    return [
        [(2 * a, 2 * b) for a, b in level]
        + [(count - 1 - 2 * a, count - 1 - 2 * b) for a, b in level]
        for level in low
    ]


def tree_mid(count):
    middle = count // 2
    left, right = tree_high(0, middle), tree_low(middle, count)
    levels = []
    for k in range(max(len(left), len(right))):
        levels.append((left[k] if k < len(left) else []) + (right[k] if k < len(right) else []))
    return levels + [[(middle, middle - 1)]]


def spread_halves(count):
    half = count // 2
    low = [[(b, a) for a, b in level] for level in reversed(tree_low(0, half))]
    return [level + [(count - 1 - a, count - 1 - b) for a, b in level] for level in low]


def attention_kernel(first_ref, q_ref, kp_ref, k_ref, vp_ref, v_ref, out_ref, k_all, v_all):
    tokens = q_ref.shape[0]
    tile = ATT_HD
    span = WINDOW + tile
    k_all[:WINDOW] = kp_ref[...]
    k_all[WINDOW:] = k_ref[...]
    v_all[:WINDOW] = vp_ref[...]
    v_all[WINDOW:] = v_ref[...]
    is_first = first_ref[0] == 0
    row = lax.broadcasted_iota(jnp.int32, (tile, span), 0)
    col = lax.broadcasted_iota(jnp.int32, (tile, span), 1)
    allowed = (col > row) & (col <= row + WINDOW)
    scale = ATT_HD**-0.5 * math.log2(math.e)
    for number in range(tokens // tile):
        start = number * tile
        s = mm(q_ref[start : start + tile], k_all[start : start + span], ((1,), (1,))) * scale
        keep = allowed
        if start < WINDOW:
            keep = keep & ((col >= WINDOW - start) | jnp.logical_not(is_first))
        s = jnp.where(keep, s, -1e30)
        w = jnp.exp2(s - jnp.max(s, axis=1, keepdims=True))
        total = jnp.sum(w, axis=1, keepdims=True)
        o = mm(w.astype(bf16), v_all[start : start + span])
        out_ref[start : start + tile] = o / total


def attention(q, kp, k, vp, v, plane):
    tokens, width = q.shape
    wide = pl.BlockSpec((tokens, ATT_HD), lambda a, s: (0, a))
    before = pl.BlockSpec((WINDOW, ATT_HD), lambda a, s: (0, a))
    return pl.pallas_call(
        attention_kernel,
        out_shape=jax.ShapeDtypeStruct((tokens, width), f32),
        grid_spec=pltpu.PrefetchScalarGridSpec(
            num_scalar_prefetch=1,
            grid=(width // ATT_HD,),
            in_specs=[wide, before, wide, before, wide],
            out_specs=wide,
            scratch_shapes=[pltpu.VMEM((WINDOW + tokens, ATT_HD), bf16)] * 2,
        ),
        compiler_params=pltpu.CompilerParams(vmem_limit_bytes=VMEM_BYTES),
        cost_estimate=pl.CostEstimate(
            flops=4 * tokens * (WINDOW + ATT_HD) * width,
            bytes_accessed=12 * tokens * width,
            transcendentals=tokens * (WINDOW + ATT_HD) * (width // ATT_HD),
        ),
    )(jnp.reshape(plane, (1,)).astype(jnp.int32), q, kp, k, vp, v)


def settle_kernel(active_ref, grad_ref, init_ref, out_ref, x_ref):
    @pl.when(active_ref[0] == 1)
    def _():
        g = grad_ref[...]
        square = jnp.sum(jnp.sum(g * g, axis=0, keepdims=True), axis=1, keepdims=True)
        x_ref[...] = (g / (jnp.sqrt(square) + 1e-06)).astype(bf16)

        @pl.loop(0, NS_ITERS)
        def _(_):
            x = x_ref[...]
            gram = mm(x, x, ((1,), (1,))).astype(bf16)
            product = mm(gram, x).astype(bf16)
            second = mm(gram, product)
            x_ref[...] = (
                quintic_first * x.astype(f32)
                + quintic_second * product.astype(f32)
                + quintic_third * second
            ).astype(bf16)

        initial = init_ref[...].astype(f32)
        updated = initial + x_ref[...].astype(f32)
        target = jnp.sqrt(jnp.sum(initial * initial, axis=0, keepdims=True))
        current = jnp.sqrt(jnp.sum(updated * updated, axis=0, keepdims=True) + 1e-06)
        out_ref[...] = (updated * (target / current)).astype(bf16)

    @pl.when(active_ref[0] == 0)
    def _():
        out_ref[...] = jnp.zeros_like(out_ref)


def renew(gradient, initial, active):
    rows, columns = gradient.shape
    vmem = pl.BlockSpec(memory_space=pltpu.VMEM)
    return pl.pallas_call(
        settle_kernel,
        out_shape=jax.ShapeDtypeStruct((rows, columns), bf16),
        in_specs=[pl.BlockSpec(memory_space=pltpu.SMEM), vmem, vmem],
        out_specs=vmem,
        scratch_shapes=[pltpu.VMEM((rows, columns), bf16)],
        compiler_params=pltpu.CompilerParams(vmem_limit_bytes=VMEM_BYTES),
        cost_estimate=pl.CostEstimate(
            flops=6 * NS_ITERS * rows * rows * columns,
            bytes_accessed=8 * rows * columns,
            transcendentals=0,
        ),
    )(jnp.reshape(active, (1,)).astype(jnp.int32), gradient, initial)


def apply_kernel(which_ref, q_ref, gate_ref, lift_ref, down_ref, att_ref, gain_ref, out_ref):
    q = q_ref[...]
    gate = mm(q, gate_ref[...])
    lift = mm(q, lift_ref[...])
    hidden = (gate / (1.0 + jnp.exp(-gate)) * lift).astype(bf16)
    result = mm(hidden, down_ref[...])
    scale = lax.rsqrt(jnp.mean(result * result, axis=1, keepdims=True) + 1e-06)
    out_ref[...] = (att_ref[...] + result * scale * gain_ref[...]).astype(bf16)


def apply_fast(q, gate, lift, down, attended, gain, which):
    tokens, width = q.shape
    rows = min(256, tokens)
    blocks = tokens // rows
    whole = pl.BlockSpec((width, width), lambda i, s: (0, 0))
    return pl.pallas_call(
        apply_kernel,
        out_shape=jax.ShapeDtypeStruct((tokens, width), bf16),
        grid_spec=pltpu.PrefetchScalarGridSpec(
            num_scalar_prefetch=1,
            grid=(blocks,),
            in_specs=[
                pl.BlockSpec((rows, width), lambda i, s: (i, 0)),
                whole,
                whole,
                whole,
                pl.BlockSpec((rows, width), lambda i, s: (s[0] * blocks + i, 0)),
                pl.BlockSpec((1, width), lambda i, s: (0, 0)),
            ],
            out_specs=pl.BlockSpec((rows, width), lambda i, s: (i, 0)),
        ),
        compiler_params=pltpu.CompilerParams(vmem_limit_bytes=VMEM_BYTES),
        cost_estimate=pl.CostEstimate(
            flops=6 * tokens * width * width,
            bytes_accessed=10 * tokens * width + 6 * width * width,
            transcendentals=tokens * width,
        ),
    )(jnp.reshape(which, (1,)).astype(jnp.int32), q, gate, lift, down, attended, gain)


def project_kernel(count, has_total, *refs):
    chunk_refs = refs[1 : 1 + count]
    w_ref = refs[1 + count]
    total_ref = refs[2 + count] if has_total else None
    out_ref, sum_ref = refs[-2:]
    step = pl.program_id(0)
    for number in range(count):

        @pl.when(step == number)
        def _(number=number):
            part = mm(chunk_refs[number][...], w_ref[...])
            if number > 0:
                part += sum_ref[...]
            elif has_total:
                part += total_ref[...]
            if number == count - 1:
                out_ref[...] = part.astype(out_ref.dtype)
            else:
                sum_ref[...] = part


def project(chunks, places, weight, total, is_last):
    count = len(chunks)
    rows, depth = chunks[0].shape
    columns = weight.shape[1]
    fixed = pl.BlockSpec((rows, depth), lambda k, s: (0, 0))
    square = pl.BlockSpec((rows, columns), lambda k, s: (0, 0))
    operands = list(chunks) + [weight]
    specs = [fixed] * count + [pl.BlockSpec((depth, columns), lambda k, s: (s[k], 0))]
    if total is not None:
        operands.append(total)
        specs.append(square)
    return pl.pallas_call(
        functools.partial(project_kernel, count, total is not None),
        out_shape=jax.ShapeDtypeStruct((rows, columns), bf16 if is_last else f32),
        grid_spec=pltpu.PrefetchScalarGridSpec(
            num_scalar_prefetch=1,
            grid=(count,),
            in_specs=specs,
            out_specs=square,
            scratch_shapes=[pltpu.VMEM((rows, columns), f32)],
        ),
        compiler_params=pltpu.CompilerParams(vmem_limit_bytes=PROJECT_BYTES),
        cost_estimate=pl.CostEstimate(
            flops=2 * count * rows * depth * columns,
            bytes_accessed=2 * count * (rows + columns) * depth + 8 * rows * columns,
            transcendentals=0,
        ),
    )(jnp.stack(places).astype(jnp.int32), *operands)


OVER_TOKENS = ((0,), (0,))


def forward(keys, gate, lift):
    gate_pre = mm(keys, gate)
    lift_pre = mm(keys, lift)
    logistic = jax.nn.sigmoid(gate_pre)
    silu = gate_pre * logistic
    hidden = (silu * lift_pre).astype(bf16)
    return hidden, lift_pre * (logistic * (1.0 + gate_pre * (1.0 - logistic))), silu


def on_device(
    queries,
    key_rows,
    value_rows,
    learning_rates,
    fast_gate,
    fast_lift,
    fast_down,
    output_gain,
    output_weight,
):
    tokens = queries.shape[0]
    group, width = fast_gate.shape[0], fast_gate.shape[1]
    context = lax.axis_size("ctx")
    columns_of = lax.axis_size("head")
    planes = context // group
    place = lax.axis_index("ctx")
    member, plane = place % group, place // group
    head_place = lax.axis_index("head")

    def to_member(array, by):
        pairs = [(i, i // group * group + (i + by) % group) for i in range(context)]
        return lax.ppermute(array, "ctx", pairs)

    def between_planes(array, pairs):
        return lax.ppermute(
            array,
            "ctx",
            [(a * group + m, b * group + m) for a, b in pairs for m in range(group)],
        )

    def head_columns(array, by):
        return lax.dynamic_slice_in_dim(array, (member + by) % group * width, width, 1)

    gate, lift, down = (
        lax.dynamic_index_in_dim(w, member, 0, keepdims=False)
        for w in (fast_gate, fast_lift, fast_down)
    )
    gain = lax.dynamic_slice_in_dim(output_gain, member * width, width, 0)[None]

    onward = [(i, i + 1) for i in range(planes - 1)]

    def in_order(blocks):
        return [pick(blocks, (member - j) % group) for j in range(group)]

    keys = [head_columns(key_rows, by) for by in range(group)]
    values = [head_columns(value_rows, by) for by in range(group)]
    asked = [head_columns(queries, by) for by in range(group)]
    rates = [
        lax.dynamic_index_in_dim(learning_rates, (member + by) % group, 0, keepdims=False)
        for by in range(group)
    ]
    keys = keys[:1] + [to_member(keys[by], by) for by in range(1, group)]
    rates = rates[:1] + [to_member(rates[by], by) for by in range(1, group)]
    values = values[:1] + [to_member(values[by], by) for by in range(1, group)]
    ordered_keys = in_order(keys)
    earlier_keys = between_planes(ordered_keys[-1][-WINDOW:], onward)
    forwards = [forward(block, gate, lift) for block in keys]
    hidden = forwards[-1][0]
    asked = asked[:1] + [to_member(after(asked[by], hidden), by) for by in range(1, group)]
    values = values[:1] + [after(block, hidden) for block in values[1:]]
    ordered_values = in_order(values)

    hiddens, slopes, silus, scaleds = [], [], [], []
    total_down = 0.0
    for by in range(group):
        hidden, slope, silu = forwards[by]
        block = values[by] if by < group - 1 else after(values[by], earlier_keys)
        scaled = (rates[by][:, None] * block.astype(f32)).astype(bf16)
        total_down = total_down + mm(hidden, scaled, OVER_TOKENS)
        slopes.append(slope)
        silus.append(silu)
        scaleds.append(scaled)
    total_gate, total_lift = 0.0, 0.0
    for by in range(group):
        scaled = scaleds[by] if by < group - 1 else after(scaleds[by], total_down)
        backward = mm(scaled, down, ((1,), (1,)))
        total_gate = total_gate + mm(keys[by], (backward * slopes[by]).astype(bf16), OVER_TOKENS)
        total_lift = total_lift + mm(keys[by], (backward * silus[by]).astype(bf16), OVER_TOKENS)

    rows = width // PIECES

    def cut(matrix):
        return [matrix[piece * rows : (piece + 1) * rows] for piece in range(PIECES)]

    def add_from(own, pairs):
        return own + between_planes(own.astype(bf16), pairs).astype(f32)

    down_levels = tree_mid(planes)
    sum_down = add_from(total_down, down_levels[0])
    odd = plane % 2 == 1
    kept = cut(jnp.where(odd, total_lift, total_gate))
    given = cut(jnp.where(odd, total_gate, total_lift).astype(bf16))
    neighbours = [(i, i ^ 1) for i in range(planes)]
    given = [between_planes(after(other, sum_down), neighbours) for other in given]
    for level in down_levels[1:]:
        sum_down = add_from(sum_down, level)
    kept = [own + got.astype(f32) for own, got in zip(kept, given)]
    met = list(kept)
    middle_plane = plane == planes // 2 - 1
    new_down = renew(after(sum_down, *met), down, middle_plane)
    for level in tree_ends(planes):
        kept = [
            after(own, new_down) + between_planes(own.astype(bf16), level).astype(f32) for own in kept
        ]

    def spread(own, pairs):
        got = between_planes(own, pairs)
        here = functools.reduce(jnp.logical_or, [plane == b for _, b in pairs])
        return jnp.where(here, got, own)

    low_plane, high_plane = plane == 0, plane == planes - 1
    new_sums = jnp.concatenate(kept)
    earlier_values = between_planes(after(ordered_values[-1][-WINDOW:], new_sums), onward)
    new_outer = renew(after(new_sums, new_down), jnp.where(low_plane, gate, lift), low_plane | high_plane)
    half = planes // 2
    swap = [(i, (i + half) % planes) for i in range(planes)]
    owners = [pair for pair in swap if pair[0] in (0, planes - 1)]
    others = [pair for pair in swap if pair not in owners]
    is_owner_swap = functools.reduce(jnp.logical_or, [plane == b for _, b in owners])
    near, far = [], []
    new_down = spread(new_down, [(b, a) for a, b in down_levels[-1]])
    near, far = [], []
    for piece, own in enumerate(cut(new_outer)):
        own = own if piece == 0 else after(own, earlier_values)
        first = between_planes(own, owners)
        passed = own
        for level in spread_halves(planes):
            got = between_planes(own, level)
            here = functools.reduce(jnp.logical_or, [plane == b for _, b in level])
            own = jnp.where(here, got, own)
            passed = got
        passed = passed if len(spread_halves(planes)) == 1 else own
        near.append(own)
        far.append((first, between_planes(passed, others)))
    for level in reversed(down_levels[:-1]):
        new_down = spread(after(new_down, *near), [(b, a) for a, b in level])

    attended = attention(
        after(jnp.concatenate(in_order(asked)), *near),
        earlier_keys,
        jnp.concatenate(ordered_keys),
        earlier_values,
        jnp.concatenate(ordered_values),
        plane,
    )
    lower = plane < half
    far = [jnp.where(is_owner_swap, after(first, attended), after(other, attended)) for first, other in far]
    new_gate = jnp.concatenate([jnp.where(lower, a, b) for a, b in zip(near, far)])
    new_lift = jnp.concatenate([jnp.where(lower, b, a) for a, b in zip(near, far)])
    bits = [1 << k for k in reversed(range(columns_of.bit_length() - 1))]

    def swapped(part, bit):
        return lax.ppermute(part, "head", [(i, i ^ bit) for i in range(columns_of)])

    def places(offsets, head):
        return [(head_place ^ o) * group + head for o in offsets]

    arrived, combined = [], None
    for by in list(range(1, group)) + [0]:
        wanted = asked[by] if combined is None else after(asked[by], combined)
        combined = apply_fast(wanted, new_gate, new_lift, new_down, attended, gain, (member - by) % group)
        if by > 0:
            arrived.append((to_member(combined, group - by), (member + by) % group))
    arrived = [(combined, member)] + arrived

    total, far_parts, far_offsets = None, [], []
    for number, (chunk, head) in enumerate(arrived):
        near_parts, near_offsets = [chunk, swapped(chunk, 1)], [0, 1]
        if total is not None:
            total = project(far_parts, far_places, output_weight, total, False)
        far_parts, far_offsets = [], []
        for bit in bits[:-1]:
            step = [swapped(part, bit) for part in [chunk] + far_parts[::2]]
            for part, offset in zip(step, [bit] + [o ^ bit for o in far_offsets[::2]]):
                far_parts += [part, swapped(part, 1)]
                far_offsets += [offset, offset ^ 1]
        far_places = places(far_offsets, head)
        total = project(near_parts, places(near_offsets, head), output_weight, total, False)
    return project(far_parts, far_places, output_weight, total, True)


def solution(mesh):
    return jax.shard_map(
        on_device,
        mesh=mesh,
        in_specs=(
            P("ctx", "head"),
            P("ctx", "head"),
            P("ctx", "head"),
            P("head", "ctx"),
            P("head", None, None),
            P("head", None, None),
            P("head", None, None),
            P("head"),
            P(None, "head"),
        ),
        out_specs=P("ctx", "head"),
        check_vma=False,
    )
```

profile of v0, /device:TPU:0, one launch (start us, length us, event | category | flops | bytes accessed | tf_op | source)
XLA Modules:
  0.0 236.6 jit_solution(15161221588861816452)
XLA Ops:
  17.3 6.6 %collective-permute-done = bf16[512,640]{1,0:T(8,128)(2,1)} collective-permute-done((bf16[512,640]{1,0:T(8,128)(2,1)}, bf16[512,640]{1,0:T(8,128)(2,1)}, u32[]{:S(2)}, u32[]{:S(2)}) %collective-permute-start) | collective-permute-done | bytes 655392 | tf_op jit(solution)/shard_map/ppermute | solution.py:304
  25.2 3.5 %collective-permute-start.4 = (bf16[512,640]{1,0:T(8,128)(2,1)S(1)}, bf16[512,640]{1,0:T(8,128)(2,1)S(1)}, u32[]{:S(2)}, u32[]{:S(2)}) collective-permute-start(bf16[512,640]{1,0:T(8,128)(2,1)S(1)} %get-tuple-element.54), channel_id=1, source_target_pairs={{0,8},{4,12},{8,16},{12,20},{16,24},{20,28},{1,9},{5,13},{9,17},{1... | collective-permute-start | bytes 1966088 | tf_op jit(solution)/shard_map/ppermute | solution.py:307
  32.5 4.0 %collective-permute-done.3 = bf16[512,640]{1,0:T(8,128)(2,1)} collective-permute-done((bf16[512,640]{1,0:T(8,128)(2,1)}, bf16[512,640]{1,0:T(8,128)(2,1)}, u32[]{:S(2)}, u32[]{:S(2)}) %collective-permute-start.3) | collective-permute-done | bytes 655392 | tf_op jit(solution)/shard_map/ppermute | solution.py:304
  42.8 4.4 %collective-permute-start.5 = (bf16[640,640]{1,0:T(8,128)(2,1)S(1)}, bf16[640,640]{1,0:T(8,128)(2,1)S(1)}, u32[]{:S(2)}, u32[]{:S(2)}) collective-permute-start(bf16[640,640]{1,0:T(8,128)(2,1)S(1)} %get-tuple-element.71), channel_id=1, source_target_pairs={{0,8},{4,12},{24,16},{28,20},{1,9},{5,13},{25,17},{29,21},{2,10},{... | collective-permute-start | bytes 2457608 | tf_op jit(solution)/shard_map/ppermute | solution.py:307
  51.3 11.5 %collective-permute-done.5 = bf16[640,640]{1,0:T(8,128)(2,1)S(1)} collective-permute-done((bf16[640,640]{1,0:T(8,128)(2,1)S(1)}, bf16[640,640]{1,0:T(8,128)(2,1)S(1)}, u32[]{:S(2)}, u32[]{:S(2)}) %collective-permute-start.5) | collective-permute-done | bytes 819232 | tf_op jit(solution)/shard_map/ppermute | solution.py:307
  67.2 7.0 %collective-permute-done.6 = bf16[320,640]{1,0:T(8,128)(2,1)S(1)} collective-permute-done((bf16[320,640]{1,0:T(8,128)(2,1)S(1)}, bf16[320,640]{1,0:T(8,128)(2,1)S(1)}, u32[]{:S(2)}, u32[]{:S(2)}) %collective-permute-start.6) | collective-permute-done | bytes 409632 | tf_op jit(solution)/shard_map/ppermute | solution.py:307
  74.3 4.4 %collective-permute-done.8 = bf16[320,640]{1,0:T(8,128)(2,1)S(1)} collective-permute-done((bf16[320,640]{1,0:T(8,128)(2,1)S(1)}, bf16[320,640]{1,0:T(8,128)(2,1)S(1)}, u32[]{:S(2)}, u32[]{:S(2)}) %collective-permute-start.8) | collective-permute-done | bytes 409632 | tf_op jit(solution)/shard_map/ppermute | solution.py:307
  82.7 17.0 %collective-permute-done.10 = bf16[320,640]{1,0:T(8,128)(2,1)S(1)} collective-permute-done((bf16[320,640]{1,0:T(8,128)(2,1)S(1)}, bf16[320,640]{1,0:T(8,128)(2,1)S(1)}, u32[]{:S(2)}, u32[]{:S(2)}) %collective-permute-start.10) | collective-permute-done | bytes 409632 | tf_op jit(solution)/shard_map/ppermute | solution.py:307
  100.0 8.1 %shard_map.92 = bf16[640,640]{1,0:T(8,128)(2,1)S(1)} custom-call(s32[1]{0:T(128)} %bitcast.5.active_ref, f32[640,640]{1,0:T(8,128)S(1)} %pad_maximum_fusion.grad_ref, bf16[640,640]{1,0:T(8,128)(2,1)S(1)} %bitcast_select_fusion.init_ref), custom_call_target="tpu_custom_call" | custom-call | flops 4718592000 | bytes 3276800 | tf_op jit(solution)/shard_map/pallas_call | solution.py:164
  111.2 8.2 %collective-permute-done.11 = bf16[320,640]{1,0:T(8,128)(2,1)S(1)} collective-permute-done((bf16[320,640]{1,0:T(8,128)(2,1)S(1)}, bf16[320,640]{1,0:T(8,128)(2,1)S(1)}, u32[]{:S(2)}, u32[]{:S(2)}) %collective-permute-start.11) | collective-permute-done | bytes 409632 | tf_op jit(solution)/shard_map/ppermute | solution.py:307
  119.5 10.1 %collective-permute-done.13.vp_ref = bf16[512,640]{1,0:T(8,128)(2,1)S(1)} collective-permute-done((bf16[512,640]{1,0:T(8,128)(2,1)S(1)}, bf16[512,640]{1,0:T(8,128)(2,1)S(1)}, u32[]{:S(2)}, u32[]{:S(2)}) %collective-permute-start.13) | collective-permute-done | bytes 655392 | tf_op jit(solution)/shard_map/ppermute | solution.py:307
  129.6 4.4 %collective-permute-start.14 = (bf16[320,640]{1,0:T(8,128)(2,1)S(1)}, bf16[320,640]{1,0:T(8,128)(2,1)S(1)}, u32[]{:S(2)}, u32[]{:S(2)}) collective-permute-start(bf16[320,640]{1,0:T(8,128)(2,1)S(1)} %get-tuple-element.35), channel_id=1, source_target_pairs={{0,8},{4,12},{24,16},{28,20},{1,9},{5,13},{25,17},{29,21},{2,10},{... | collective-permute-start | bytes 1228808 | tf_op jit(solution)/shard_map/ppermute | solution.py:307
  136.7 5.5 %collective-permute-start.16 = (bf16[320,640]{1,0:T(8,128)(2,1)S(1)}, bf16[320,640]{1,0:T(8,128)(2,1)S(1)}, u32[]{:S(2)}, u32[]{:S(2)}) collective-permute-start(bf16[320,640]{1,0:T(8,128)(2,1)S(1)} %get-tuple-element.35), channel_id=1, source_target_pairs={{0,16},{4,20},{24,8},{28,12},{1,17},{5,21},{25,9},{29,13},{2,18},{... | collective-permute-start | bytes 1228808 | tf_op jit(solution)/shard_map/ppermute | solution.py:307
  146.6 14.5 %shard_map.93.att_ref = f32[1024,640]{1,0:T(8,128)S(1)} custom-call(s32[1]{0:T(128)} %bitcast.10.first_ref, bf16[1024,640]{1,0:T(8,128)(2,1)S(1)} %pad_maximum_fusion.1.q_ref, bf16[512,640]{1,0:T(8,128)(2,1)S(1)} %collective-permute-done.4.kp_ref, bf16[1024,640]{1,0:T(8,128)(2,1)S(1)} %pad_maximum_fusion.2.k_ref, ...), custom_call_target="tpu_custom_call" | custom-call | flops 1677721600 | bytes 7864320 | tf_op jit(solution)/shard_map/pallas_call | solution.py:112
  161.1 3.5 %collective-permute-done.15 = bf16[320,640]{1,0:T(8,128)(2,1)S(1)} collective-permute-done((bf16[320,640]{1,0:T(8,128)(2,1)S(1)}, bf16[320,640]{1,0:T(8,128)(2,1)S(1)}, u32[]{:S(2)}, u32[]{:S(2)}) %collective-permute-start.15) | collective-permute-done | bytes 409632 | tf_op jit(solution)/shard_map/ppermute | solution.py:307
  164.7 6.2 %collective-permute-done.17 = bf16[320,640]{1,0:T(8,128)(2,1)S(1)} collective-permute-done((bf16[320,640]{1,0:T(8,128)(2,1)S(1)}, bf16[320,640]{1,0:T(8,128)(2,1)S(1)}, u32[]{:S(2)}, u32[]{:S(2)}) %collective-permute-start.17) | collective-permute-done | bytes 409632 | tf_op jit(solution)/shard_map/ppermute | solution.py:307
  171.3 5.1 %collective-permute-done.19 = bf16[640,640]{1,0:T(8,128)(2,1)S(1)} collective-permute-done((bf16[640,640]{1,0:T(8,128)(2,1)S(1)}, bf16[640,640]{1,0:T(8,128)(2,1)S(1)}, u32[]{:S(2)}, u32[]{:S(2)}) %collective-permute-start.19) | collective-permute-done | bytes 819232 | tf_op jit(solution)/shard_map/ppermute | solution.py:307
  183.7 6.0 %collective-permute-done.20.refs_1_ = bf16[512,640]{1,0:T(8,128)(2,1)S(1)} collective-permute-done((bf16[512,640]{1,0:T(8,128)(2,1)S(1)}, bf16[512,640]{1,0:T(8,128)(2,1)S(1)}, u32[]{:S(2)}, u32[]{:S(2)}) %collective-permute-start.20) | collective-permute-done | bytes 655392 | tf_op jit(solution)/shard_map/ppermute | solution.py:304
  191.2 6.7 %collective-permute-done.24.refs_1_ = bf16[512,640]{1,0:T(8,128)(2,1)S(1)} collective-permute-done((bf16[512,640]{1,0:T(8,128)(2,1)S(1)}, bf16[512,640]{1,0:T(8,128)(2,1)S(1)}, u32[]{:S(2)}, u32[]{:S(2)}) %collective-permute-start.24) | collective-permute-done | bytes 655392 | tf_op jit(solution)/shard_map/ppermute | solution.py:435
  199.1 6.0 %collective-permute-done.21.refs_1_ = bf16[512,640]{1,0:T(8,128)(2,1)} collective-permute-done((bf16[512,640]{1,0:T(8,128)(2,1)S(1)}, bf16[512,640]{1,0:T(8,128)(2,1)}, u32[]{:S(2)}, u32[]{:S(2)}) %collective-permute-start.21) | collective-permute-done | bytes 655392 | tf_op jit(solution)/shard_map/ppermute | solution.py:435
  207.2 6.4 %shard_map.96.refs_4_ = f32[512,1280]{1,0:T(8,128)} custom-call(s32[2]{0:T(128)} %pad_add_fusion.3.refs_0_, bf16[512,640]{1,0:T(8,128)(2,1)} %copy-done.2, bf16[512,640]{1,0:T(8,128)(2,1)} %copy-done.12, bf16[5120,1280]{1,0:T(8,128)(2,1)} %refs_3_.7), custom_call_target="tpu_custom_call" | custom-call | flops 1677721600 | bytes 9830400 | tf_op jit(solution)/shard_map/pallas_call | solution.py:251
  213.5 7.2 %shard_map.97.refs_4_ = f32[512,1280]{1,0:T(8,128)} custom-call(s32[2]{0:T(128)} %pad_add_fusion.2.refs_0_, bf16[512,640]{1,0:T(8,128)(2,1)} %copy-done.10, bf16[512,640]{1,0:T(8,128)(2,1)} %collective-permute-done.25.refs_2_, bf16[5120,1280]{1,0:T(8,128)(2,1)} %refs_3_.7, f32[512,1280]{1,0:T(8,128)} %shard_map.96.refs_4_), custom_call_target="tpu_custom_call" | custom-call | flops 1677721600 | bytes 9830400 | tf_op jit(solution)/shard_map/pallas_call | solution.py:251
  221.6 7.2 %shard_map.98.refs_4_ = f32[512,1280]{1,0:T(8,128)} custom-call(s32[2]{0:T(128)} %get-tuple-element.74.refs_0_, bf16[512,640]{1,0:T(8,128)(2,1)} %copy-done.9, bf16[512,640]{1,0:T(8,128)(2,1)} %copy-done.11, bf16[5120,1280]{1,0:T(8,128)(2,1)} %refs_3_.7, f32[512,1280]{1,0:T(8,128)} %shard_map.97.refs_4_), custom_call_target="tpu_custom_call" | custom-call | flops 1677721600 | bytes 9830400 | tf_op jit(solution)/shard_map/pallas_call | solution.py:251
  229.7 6.9 %shard_map.99 = bf16[512,1280]{1,0:T(8,128)(2,1)} custom-call(s32[2]{0:T(128)} %get-tuple-element.73.refs_0_, bf16[512,640]{1,0:T(8,128)(2,1)} %collective-permute-done.21.refs_1_, bf16[512,640]{1,0:T(8,128)(2,1)} %copy-done.13, bf16[5120,1280]{1,0:T(8,128)(2,1)} %refs_3_.7, f32[512,1280]{1,0:T(8,128)} %shard_map.98.refs_4_), custom_call_target="tpu_custom_call" | custom-call | flops 1677721600 | bytes 9830400 | tf_op jit(solution)/shard_map/pallas_call | solution.py:251
  (116 shorter events, 65.7 us)
Async XLA Ops:
  0.8 39.2 %collective-permute-start.2 = (f32[512]{0:T(512)S(1)}, f32[512]{0:T(512)S(1)}, u32[]{:S(2)}, u32[]{:S(2)}) collective-permute-start(f32[512]{0:T(512)S(1)} %bitcast.42), channel_id=1, source_target_pairs={{0,4},{4,0},{8,12},{12,8},{16,20},{20,16},{24,28},{28,24},{1,5},{5... | collective-permute-start | bytes 6152 | tf_op jit(solution)/shard_map/ppermute | solution.py:304
  5.9 18.0 %collective-permute-start = (bf16[512,640]{1,0:T(8,128)(2,1)}, bf16[512,640]{1,0:T(8,128)(2,1)}, u32[]{:S(2)}, u32[]{:S(2)}) collective-permute-start(bf16[512,640]{1,0:T(8,128)(2,1)} %constant_dynamic-slice_fusion.4), channel_id=1, source_target_pairs={{0,4},{4,0},{8,12},{12,8},{16,20},{20,16},{24,28},{28,24},{1,5},{5... | collective-permute-start | bytes 1966088 | tf_op jit(solution)/shard_map/ppermute | solution.py:304
  6.8 29.6 %collective-permute-start.3 = (bf16[512,640]{1,0:T(8,128)(2,1)}, bf16[512,640]{1,0:T(8,128)(2,1)}, u32[]{:S(2)}, u32[]{:S(2)}) collective-permute-start(bf16[512,640]{1,0:T(8,128)(2,1)} %constant_dynamic-slice_fusion.1), channel_id=1, source_target_pairs={{0,4},{4,0},{8,12},{12,8},{16,20},{20,16},{24,28},{28,24},{1,5},{5... | collective-permute-start | bytes 1966088 | tf_op jit(solution)/shard_map/ppermute | solution.py:304
  25.2 14.8 %collective-permute-start.4 = (bf16[512,640]{1,0:T(8,128)(2,1)S(1)}, bf16[512,640]{1,0:T(8,128)(2,1)S(1)}, u32[]{:S(2)}, u32[]{:S(2)}) collective-permute-start(bf16[512,640]{1,0:T(8,128)(2,1)S(1)} %get-tuple-element.54), channel_id=1, source_target_pairs={{0,8},{4,12},{8,16},{12,20},{16,24},{20,28},{1,9},{5,13},{9,17},{1... | collective-permute-start | bytes 1966088 | tf_op jit(solution)/shard_map/ppermute | solution.py:307
  42.8 20.0 %collective-permute-start.5 = (bf16[640,640]{1,0:T(8,128)(2,1)S(1)}, bf16[640,640]{1,0:T(8,128)(2,1)S(1)}, u32[]{:S(2)}, u32[]{:S(2)}) collective-permute-start(bf16[640,640]{1,0:T(8,128)(2,1)S(1)} %get-tuple-element.71), channel_id=1, source_target_pairs={{0,8},{4,12},{24,16},{28,20},{1,9},{5,13},{25,17},{29,21},{2,10},{... | collective-permute-start | bytes 2457608 | tf_op jit(solution)/shard_map/ppermute | solution.py:307
  65.6 13.1 %collective-permute-start.8 = (bf16[320,640]{1,0:T(8,128)(2,1)S(1)}, bf16[320,640]{1,0:T(8,128)(2,1)S(1)}, u32[]{:S(2)}, u32[]{:S(2)}) collective-permute-start(bf16[320,640]{1,0:T(8,128)(2,1)S(1)} %get-tuple-element.29), channel_id=1, source_target_pairs={{0,8},{4,12},{8,0},{12,4},{16,24},{20,28},{24,16},{28,20},{1,9},{5... | collective-permute-start | bytes 1228808 | tf_op jit(solution)/shard_map/ppermute | solution.py:307
  65.7 15.9 %collective-permute-start.7 = (bf16[640,640]{1,0:T(8,128)(2,1)S(1)}, bf16[640,640]{1,0:T(8,128)(2,1)S(1)}, u32[]{:S(2)}, u32[]{:S(2)}) collective-permute-start(bf16[640,640]{1,0:T(8,128)(2,1)S(1)} %get-tuple-element.49), channel_id=1, source_target_pairs={{16,8},{20,12},{17,9},{21,13},{18,10},{22,14},{19,11},{23,15}} | collective-permute-start | bytes 2457608 | tf_op jit(solution)/shard_map/ppermute | solution.py:307
  66.5 44.4 %collective-permute-start.1 = (bf16[512,640]{1,0:T(8,128)(2,1)S(1)}, bf16[512,640]{1,0:T(8,128)(2,1)S(1)}, u32[]{:S(2)}, u32[]{:S(2)}) collective-permute-start(bf16[512,640]{1,0:T(8,128)(2,1)S(1)} %constant_dynamic-slice_fusion.5), channel_id=1, source_target_pairs={{0,4},{4,0},{8,12},{12,8},{16,20},{20,16},{24,28},{28,24},{1,5},{5... | collective-permute-start | bytes 1966088 | tf_op jit(solution)/shard_map/ppermute | solution.py:304
  78.9 20.9 %collective-permute-start.9 = (bf16[320,640]{1,0:T(8,128)(2,1)S(1)}, bf16[320,640]{1,0:T(8,128)(2,1)S(1)}, u32[]{:S(2)}, u32[]{:S(2)}) collective-permute-start(bf16[320,640]{1,0:T(8,128)(2,1)S(1)} %get-tuple-element.45), channel_id=1, source_target_pairs={{16,0},{20,4},{8,24},{12,28},{17,1},{21,5},{9,25},{13,29},{18,2},{... | collective-permute-start | bytes 1228808 | tf_op jit(solution)/shard_map/ppermute | solution.py:307
  80.2 19.5 %collective-permute-start.10 = (bf16[320,640]{1,0:T(8,128)(2,1)S(1)}, bf16[320,640]{1,0:T(8,128)(2,1)S(1)}, u32[]{:S(2)}, u32[]{:S(2)}) collective-permute-start(bf16[320,640]{1,0:T(8,128)(2,1)S(1)} %get-tuple-element.55), channel_id=1, source_target_pairs={{16,0},{20,4},{8,24},{12,28},{17,1},{21,5},{9,25},{13,29},{18,2},{... | collective-permute-start | bytes 1228808 | tf_op jit(solution)/shard_map/ppermute | solution.py:307
  82.0 60.2 %collective-permute-start.18 = (bf16[640,640]{1,0:T(8,128)(2,1)S(1)}, bf16[640,640]{1,0:T(8,128)(2,1)S(1)}, u32[]{:S(2)}, u32[]{:S(2)}) collective-permute-start(bf16[640,640]{1,0:T(8,128)(2,1)S(1)} %shard_map.91), channel_id=1, source_target_pairs={{8,16},{12,20},{9,17},{13,21},{10,18},{14,22},{11,19},{15,23}} | collective-permute-start | bytes 2457608 | tf_op jit(solution)/shard_map/ppermute | solution.py:307
  109.5 20.1 %collective-permute-start.13 = (bf16[512,640]{1,0:T(8,128)(2,1)S(1)}, bf16[512,640]{1,0:T(8,128)(2,1)S(1)}, u32[]{:S(2)}, u32[]{:S(2)}) collective-permute-start(bf16[512,640]{1,0:T(8,128)(2,1)S(1)} %get-tuple-element.34), channel_id=1, source_target_pairs={{0,8},{4,12},{8,16},{12,20},{16,24},{20,28},{1,9},{5,13},{9,17},{1... | collective-permute-start | bytes 1966088 | tf_op jit(solution)/shard_map/ppermute | solution.py:307
  129.6 14.3 %collective-permute-start.14 = (bf16[320,640]{1,0:T(8,128)(2,1)S(1)}, bf16[320,640]{1,0:T(8,128)(2,1)S(1)}, u32[]{:S(2)}, u32[]{:S(2)}) collective-permute-start(bf16[320,640]{1,0:T(8,128)(2,1)S(1)} %get-tuple-element.35), channel_id=1, source_target_pairs={{0,8},{4,12},{24,16},{28,20},{1,9},{5,13},{25,17},{29,21},{2,10},{... | collective-permute-start | bytes 1228808 | tf_op jit(solution)/shard_map/ppermute | solution.py:307
  134.1 30.6 %collective-permute-start.12 = (bf16[320,640]{1,0:T(8,128)(2,1)S(1)}, bf16[320,640]{1,0:T(8,128)(2,1)S(1)}, u32[]{:S(2)}, u32[]{:S(2)}) collective-permute-start(bf16[320,640]{1,0:T(8,128)(2,1)S(1)} %slice.28), channel_id=1, source_target_pairs={{0,16},{4,20},{24,8},{28,12},{1,17},{5,21},{25,9},{29,13},{2,18},{... | collective-permute-start | bytes 1228808 | tf_op jit(solution)/shard_map/ppermute | solution.py:307
  135.4 29.3 %collective-permute-start.15 = (bf16[320,640]{1,0:T(8,128)(2,1)S(1)}, bf16[320,640]{1,0:T(8,128)(2,1)S(1)}, u32[]{:S(2)}, u32[]{:S(2)}) collective-permute-start(bf16[320,640]{1,0:T(8,128)(2,1)S(1)} %collective-permute-done.11), channel_id=1, source_target_pairs={{8,24},{12,28},{16,0},{20,4},{9,25},{13,29},{17,1},{21,5},{10,26},... | collective-permute-start | bytes 1228808 | tf_op jit(solution)/shard_map/ppermute | solution.py:307
  136.7 24.4 %collective-permute-start.16 = (bf16[320,640]{1,0:T(8,128)(2,1)S(1)}, bf16[320,640]{1,0:T(8,128)(2,1)S(1)}, u32[]{:S(2)}, u32[]{:S(2)}) collective-permute-start(bf16[320,640]{1,0:T(8,128)(2,1)S(1)} %get-tuple-element.35), channel_id=1, source_target_pairs={{0,16},{4,20},{24,8},{28,12},{1,17},{5,21},{25,9},{29,13},{2,18},{... | collective-permute-start | bytes 1228808 | tf_op jit(solution)/shard_map/ppermute | solution.py:307
  143.9 27.0 %collective-permute-start.17 = (bf16[320,640]{1,0:T(8,128)(2,1)S(1)}, bf16[320,640]{1,0:T(8,128)(2,1)S(1)}, u32[]{:S(2)}, u32[]{:S(2)}) collective-permute-start(bf16[320,640]{1,0:T(8,128)(2,1)S(1)} %collective-permute-done.14), channel_id=1, source_target_pairs={{8,24},{12,28},{16,0},{20,4},{9,25},{13,29},{17,1},{21,5},{10,26},... | collective-permute-start | bytes 1228808 | tf_op jit(solution)/shard_map/ppermute | solution.py:307
  145.2 31.2 %collective-permute-start.19 = (bf16[640,640]{1,0:T(8,128)(2,1)S(1)}, bf16[640,640]{1,0:T(8,128)(2,1)S(1)}, u32[]{:S(2)}, u32[]{:S(2)}) collective-permute-start(bf16[640,640]{1,0:T(8,128)(2,1)S(1)} %broadcast_select_fusion), channel_id=1, source_target_pairs={{8,0},{12,4},{16,24},{20,28},{9,1},{13,5},{17,25},{21,29},{10,2},{... | collective-permute-start | bytes 2457608 | tf_op jit(solution)/shard_map/ppermute | solution.py:307
  182.1 15.8 %collective-permute-start.24 = (bf16[512,640]{1,0:T(8,128)(2,1)S(1)}, bf16[512,640]{1,0:T(8,128)(2,1)S(1)}, u32[]{:S(2)}, u32[]{:S(2)}) collective-permute-start(bf16[512,640]{1,0:T(8,128)(2,1)S(1)} %shard_map.95.refs_1_), channel_id=1, source_target_pairs={{0,2},{1,3},{2,0},{3,1},{4,6},{5,7},{6,4},{7,5},{8,10},{9,11},{10,... | collective-permute-start | bytes 1966088 | tf_op jit(solution)/shard_map/ppermute | solution.py:435
  189.7 15.4 %collective-permute-start.21 = (bf16[512,640]{1,0:T(8,128)(2,1)S(1)}, bf16[512,640]{1,0:T(8,128)(2,1)}, u32[]{:S(2)}, u32[]{:S(2)}) collective-permute-start(bf16[512,640]{1,0:T(8,128)(2,1)S(1)} %collective-permute-done.20.refs_1_), channel_id=1, source_target_pairs={{0,2},{1,3},{2,0},{3,1},{4,6},{5,7},{6,4},{7,5},{8,10},{9,11},{10,... | collective-permute-start | bytes 1966088 | tf_op jit(solution)/shard_map/ppermute | solution.py:435
  191.2 15.1 %collective-permute-start.26 = (bf16[512,640]{1,0:T(8,128)(2,1)S(1)}, bf16[512,640]{1,0:T(8,128)(2,1)S(1)}, u32[]{:S(2)}, u32[]{:S(2)}) collective-permute-start(bf16[512,640]{1,0:T(8,128)(2,1)S(1)} %shard_map.95.refs_1_), channel_id=1, source_target_pairs={{0,1},{1,0},{2,3},{3,2},{4,5},{5,4},{6,7},{7,6},{8,9},{9,8},{10,11... | collective-permute-start | bytes 1966088 | tf_op jit(solution)/shard_map/ppermute | solution.py:435
  197.9 15.6 %collective-permute-start.25 = (bf16[512,640]{1,0:T(8,128)(2,1)S(1)}, bf16[512,640]{1,0:T(8,128)(2,1)}, u32[]{:S(2)}, u32[]{:S(2)}) collective-permute-start(bf16[512,640]{1,0:T(8,128)(2,1)S(1)} %collective-permute-done.24.refs_1_), channel_id=1, source_target_pairs={{0,1},{1,0},{2,3},{3,2},{4,5},{5,4},{6,7},{7,6},{8,9},{9,8},{10,11... | collective-permute-start | bytes 1966088 | tf_op jit(solution)/shard_map/ppermute | solution.py:435
  197.9 22.8 %collective-permute-start.23 = (bf16[512,640]{1,0:T(8,128)(2,1)S(1)}, bf16[512,640]{1,0:T(8,128)(2,1)S(1)}, u32[]{:S(2)}, u32[]{:S(2)}) collective-permute-start(bf16[512,640]{1,0:T(8,128)(2,1)S(1)} %collective-permute-done.20.refs_1_), channel_id=1, source_target_pairs={{0,1},{1,0},{2,3},{3,2},{4,5},{5,4},{6,7},{7,6},{8,9},{9,8},{10,11... | collective-permute-start | bytes 1966088 | tf_op jit(solution)/shard_map/ppermute | solution.py:435
  205.0 23.8 %collective-permute-start.22 = (bf16[512,640]{1,0:T(8,128)(2,1)}, bf16[512,640]{1,0:T(8,128)(2,1)S(1)}, u32[]{:S(2)}, u32[]{:S(2)}) collective-permute-start(bf16[512,640]{1,0:T(8,128)(2,1)} %collective-permute-done.21.refs_1_), channel_id=1, source_target_pairs={{0,1},{1,0},{2,3},{3,2},{4,5},{5,4},{6,7},{7,6},{8,9},{9,8},{10,11... | collective-permute-start | bytes 1966088 | tf_op jit(solution)/shard_map/ppermute | solution.py:435
  (18 other events, 130.9 us)
where the time goes:
time: 238 us; the launch traced here: 237 us
  waiting for transfers between devices  106 us (45%)
  Pallas kernels  55.5 us (23%)
  starting transfers between devices  42.1 us (18%)
  matrix products  14.1 us (6%)
  local copies, waits for them, and re-layouts  9.8 us (4%)
  other arithmetic  8.45 us (4%)
    ppermute x16, waiting for transfers between devices, between_planes(): lax.ppermute(array, 'ctx', [(a * group + m, b * group + m) for a, b in pa...  76.9 us
    ppermute x16, starting transfers between devices, between_planes(): lax.ppermute(array, 'ctx', [(a * group + m, b * group + m) for a, b in pa...  32.3 us
    pallas_call x4, Pallas kernels, project(): pl.pallas_call(functools.partial(project_kernel, count, total is not None...  27.7 us
    ppermute x5, waiting for transfers between devices, to_member(): return lax.ppermute(array, 'ctx', pairs)  16.6 us
    pallas_call x1, Pallas kernels, attention(): pl.pallas_call(attention_kernel, out_shape=jax.ShapeDtypeStruct((tokens,...  14.5 us
    dot_general x12, matrix products, mm(): return lax.dot_general(a, b, (dims, ((), ())), preferred_element_type=f32)  14.1 us
    ppermute x6, waiting for transfers between devices, swapped(): return lax.ppermute(part, 'head', [(i, i ^ bit) for i in range(columns_of)])  12.7 us
    pallas_call x2, Pallas kernels, renew(): pl.pallas_call(settle_kernel, out_shape=jax.ShapeDtypeStruct((rows, colum...  8.32 us
  transfers between devices with their start and end apart: 27, of which 16 were waited for; matrix products, arithmetic and copies ran while one was open for 10% of the time, Pallas kernels for 19%

commit v1 on v0

--- a/solution.py
+++ b/solution.py
@@ -13,7 +13,7 @@
 NS_ITERS = 3
 PIECES = 2
 VMEM_BYTES = 24 * 1024 * 1024
-PROJECT_BYTES = 58 * 1024 * 1024
+PROJECT_BYTES = 32 * 1024 * 1024
 
 quintic_first = 3.4445
 quintic_second = -4.775
@@ -216,55 +216,57 @@
     )(jnp.reshape(which, (1,)).astype(jnp.int32), q, gate, lift, down, attended, gain)
 
 
-def project_kernel(count, has_total, *refs):
-    chunk_refs = refs[1 : 1 + count]
-    w_ref = refs[1 + count]
-    total_ref = refs[2 + count] if has_total else None
-    out_ref, sum_ref = refs[-2:]
-    step = pl.program_id(0)
+def project_kernel(offsets, group, has_total, spot_ref, w_ref, *refs):
+    count = len(offsets)
+    chunk_refs = refs[:count]
+    total_ref = refs[count] if has_total else None
+    out_ref, sum_ref, w_rows, arrived = refs[-4:]
+    depth = w_rows.shape[1]
+    copies = []
+    for number, offset in enumerate(offsets):
+        start = ((spot_ref[0] ^ offset) * group + spot_ref[1]) * depth
+        copy = pltpu.make_async_copy(
+            w_ref.at[pl.ds(pl.multiple_of(start, depth), depth)], w_rows.at[number], arrived.at[number]
+        )
+        copy.start()
+        copies.append(copy)
     for number in range(count):
-
-        @pl.when(step == number)
-        def _(number=number):
-            part = mm(chunk_refs[number][...], w_ref[...])
-            if number > 0:
-                part += sum_ref[...]
-            elif has_total:
-                part += total_ref[...]
-            if number == count - 1:
-                out_ref[...] = part.astype(out_ref.dtype)
-            else:
-                sum_ref[...] = part
-
-
-def project(chunks, places, weight, total, is_last):
+        copies[number].wait()
+        part = mm(chunk_refs[number][...], w_rows[number])
+        if number > 0:
+            part += sum_ref[...]
+        elif has_total:
+            part += total_ref[...]
+        if number == count - 1:
+            out_ref[...] = part.astype(out_ref.dtype)
+        else:
+            sum_ref[...] = part
+
+
+def project(chunks, offsets, group, spot, weight, total, is_last):
     count = len(chunks)
     rows, depth = chunks[0].shape
     columns = weight.shape[1]
-    fixed = pl.BlockSpec((rows, depth), lambda k, s: (0, 0))
-    square = pl.BlockSpec((rows, columns), lambda k, s: (0, 0))
-    operands = list(chunks) + [weight]
-    specs = [fixed] * count + [pl.BlockSpec((depth, columns), lambda k, s: (s[k], 0))]
-    if total is not None:
-        operands.append(total)
-        specs.append(square)
+    vmem = pl.BlockSpec(memory_space=pltpu.VMEM)
+    operands = [spot, weight] + list(chunks) + ([] if total is None else [total])
     return pl.pallas_call(
-        functools.partial(project_kernel, count, total is not None),
+        functools.partial(project_kernel, offsets, group, total is not None),
         out_shape=jax.ShapeDtypeStruct((rows, columns), bf16 if is_last else f32),
-        grid_spec=pltpu.PrefetchScalarGridSpec(
-            num_scalar_prefetch=1,
-            grid=(count,),
-            in_specs=specs,
-            out_specs=square,
-            scratch_shapes=[pltpu.VMEM((rows, columns), f32)],
-        ),
+        in_specs=[pl.BlockSpec(memory_space=pltpu.SMEM), pl.BlockSpec(memory_space=pltpu.HBM)]
+        + [vmem] * (len(operands) - 2),
+        out_specs=vmem,
+        scratch_shapes=[
+            pltpu.VMEM((rows, columns), f32),
+            pltpu.VMEM((count, depth, columns), bf16),
+            pltpu.SemaphoreType.DMA((count,)),
+        ],
         compiler_params=pltpu.CompilerParams(vmem_limit_bytes=PROJECT_BYTES),
         cost_estimate=pl.CostEstimate(
             flops=2 * count * rows * depth * columns,
             bytes_accessed=2 * count * (rows + columns) * depth + 8 * rows * columns,
             transcendentals=0,
         ),
-    )(jnp.stack(places).astype(jnp.int32), *operands)
+    )(*operands)
 
 
 OVER_TOKENS = ((0,), (0,))
@@ -340,7 +342,6 @@
     hidden = forwards[-1][0]
     asked = asked[:1] + [to_member(after(asked[by], hidden), by) for by in range(1, group)]
     values = values[:1] + [after(block, hidden) for block in values[1:]]
-    ordered_values = in_order(values)
 
     hiddens, slopes, silus, scaleds = [], [], [], []
     total_down = 0.0
@@ -359,6 +360,10 @@
         total_gate = total_gate + mm(keys[by], (backward * slopes[by]).astype(bf16), OVER_TOKENS)
         total_lift = total_lift + mm(keys[by], (backward * silus[by]).astype(bf16), OVER_TOKENS)
 
+    ordered_values = in_order([after(block, total_down) for block in values])
+    window_values = ordered_values[-1][-WINDOW:]
+    values_early = between_planes(window_values, onward[1:])
+
     rows = width // PIECES
 
     def cut(matrix):
@@ -374,12 +379,15 @@
     given = cut(jnp.where(odd, total_gate, total_lift).astype(bf16))
     neighbours = [(i, i ^ 1) for i in range(planes)]
     given = [between_planes(after(other, sum_down), neighbours) for other in given]
+    first_sum = sum_down
     for level in down_levels[1:]:
         sum_down = add_from(sum_down, level)
     kept = [own + got.astype(f32) for own, got in zip(kept, given)]
     met = list(kept)
+    values_first = between_planes(after(window_values, first_sum), onward[:1])
+    earlier_values = jnp.where(plane == 1, values_first, values_early)
     middle_plane = plane == planes // 2 - 1
-    new_down = renew(after(sum_down, *met), down, middle_plane)
+    new_down = renew(after(sum_down, values_first, *met), down, middle_plane)
     for level in tree_ends(planes):
         kept = [
             after(own, new_down) + between_planes(own.astype(bf16), level).astype(f32) for own in kept
@@ -392,7 +400,6 @@
 
     low_plane, high_plane = plane == 0, plane == planes - 1
     new_sums = jnp.concatenate(kept)
-    earlier_values = between_planes(after(ordered_values[-1][-WINDOW:], new_sums), onward)
     new_outer = renew(after(new_sums, new_down), jnp.where(low_plane, gate, lift), low_plane | high_plane)
     half = planes // 2
     swap = [(i, (i + half) % planes) for i in range(planes)]
@@ -402,8 +409,7 @@
     near, far = [], []
     new_down = spread(new_down, [(b, a) for a, b in down_levels[-1]])
     near, far = [], []
-    for piece, own in enumerate(cut(new_outer)):
-        own = own if piece == 0 else after(own, earlier_values)
+    for own in cut(new_outer):
         first = between_planes(own, owners)
         passed = own
         for level in spread_halves(planes):
@@ -434,9 +440,6 @@
     def swapped(part, bit):
         return lax.ppermute(part, "head", [(i, i ^ bit) for i in range(columns_of)])
 
-    def places(offsets, head):
-        return [(head_place ^ o) * group + head for o in offsets]
-
     arrived, combined = [], None
     for by in list(range(1, group)) + [0]:
         wanted = asked[by] if combined is None else after(asked[by], combined)
@@ -445,20 +448,20 @@
             arrived.append((to_member(combined, group - by), (member + by) % group))
     arrived = [(combined, member)] + arrived
 
-    total, far_parts, far_offsets = None, [], []
+    total = None
     for number, (chunk, head) in enumerate(arrived):
-        near_parts, near_offsets = [chunk, swapped(chunk, 1)], [0, 1]
-        if total is not None:
-            total = project(far_parts, far_places, output_weight, total, False)
-        far_parts, far_offsets = [], []
-        for bit in bits[:-1]:
-            step = [swapped(part, bit) for part in [chunk] + far_parts[::2]]
-            for part, offset in zip(step, [bit] + [o ^ bit for o in far_offsets[::2]]):
-                far_parts += [part, swapped(part, 1)]
-                far_offsets += [offset, offset ^ 1]
-        far_places = places(far_offsets, head)
-        total = project(near_parts, places(near_offsets, head), output_weight, total, False)
-    return project(far_parts, far_places, output_weight, total, True)
+        parts = [chunk]
+        for bit in bits:
+            got = [swapped(part, bit) for part in parts]
+            if total is not None and bit == bits[0]:
+                got = [after(part, total) for part in got]
+            parts = [p for pair in zip(parts, got) for p in pair]
+        offsets = [0]
+        for bit in bits:
+            offsets = [p for o in offsets for p in (o, o ^ bit)]
+        spot = jnp.stack([head_place, head]).astype(jnp.int32)
+        total = project(parts, offsets, group, spot, output_weight, total, number == len(arrived) - 1)
+    return total
 
 
 def solution(mesh):

time: 238 us -> 207 us (0.87)
  waiting for transfers between devices: 106 us -> 82.8 us
  Pallas kernels: 55.5 us -> 43 us
  local copies, waits for them, and re-layouts: 9.8 us -> 16.9 us
  other arithmetic: 8.45 us -> 4.35 us
    ppermute x16 -> x17, waiting for transfers between devices: 76.9 us -> 59.2 us  [between_planes(): lax.ppermute(array, 'ctx', [(a * group + m, b * group + m) for a, b in pa...]
    pallas_call x4 -> x2, Pallas kernels: 27.7 us -> 15.5 us  [project(): pl.pallas_call(functools.partial(project_kernel, offsets, group, total is...]
    ppermute x5, waiting for transfers between devices: 16.6 us -> 10.2 us  [to_member(): return lax.ppermute(array, 'ctx', pairs)]
    unnamed x30 -> x18, local copies, waits for them, and re-layouts: 5.65 us -> 11.6 us
    ppermute x16 -> x17, starting transfers between devices: 32.3 us -> 35.2 us  [between_planes(): lax.ppermute(array, 'ctx', [(a * group + m, b * group + m) for a, b in pa...]
  transfers between devices with their start and end apart: 27 -> 28, of which waited for: 16 -> 17; matrix products, arithmetic and copies ran while one was open for 10% -> 12% of each run, Pallas kernels for 19% -> 15%
where the time goes in v1:
time: 207 us; the launch traced here: 206 us
  waiting for transfers between devices  82.8 us (40%)
  starting transfers between devices  43.1 us (21%)
  Pallas kernels  43 us (21%)
  local copies, waits for them, and re-layouts  16.9 us (8%)
  matrix products  15.4 us (7%)
  other arithmetic  4.35 us (2%)
    ppermute x17, waiting for transfers between devices, between_planes(): lax.ppermute(array, 'ctx', [(a * group + m, b * group + m) for a, b in pa...  59.2 us
    ppermute x17, starting transfers between devices, between_planes(): lax.ppermute(array, 'ctx', [(a * group + m, b * group + m) for a, b in pa...  35.2 us
    pallas_call x2, Pallas kernels, project(): pl.pallas_call(functools.partial(project_kernel, offsets, group, total is...  15.5 us
    dot_general x12, matrix products, mm(): return lax.dot_general(a, b, (dims, ((), ())), preferred_element_type=f32)  15.4 us
    pallas_call x1, Pallas kernels, attention(): pl.pallas_call(attention_kernel, out_shape=jax.ShapeDtypeStruct((tokens,...  14.3 us
    ppermute x6, waiting for transfers between devices, swapped(): return lax.ppermute(part, 'head', [(i, i ^ bit) for i in range(columns_of)])  13.4 us
    unnamed x18, local copies, waits for them, and re-layouts  11.6 us
    ppermute x5, waiting for transfers between devices, to_member(): return lax.ppermute(array, 'ctx', pairs)  10.2 us
  transfers between devices with their start and end apart: 28, of which 17 were waited for; matrix products, arithmetic and copies ran while one was open for 12% of the time, Pallas kernels for 15%

profile of v1, /device:TPU:0, one launch (start us, length us, event | category | flops | bytes accessed | tf_op | source)
XLA Modules:
  0.0 206.3 jit_solution(9478694157322017840)
XLA Ops:
  0.8 3.0 %collective-permute-start.2 = (f32[512]{0:T(512)S(1)}, f32[512]{0:T(512)S(1)}, u32[]{:S(2)}, u32[]{:S(2)}) collective-permute-start(f32[512]{0:T(512)S(1)} %bitcast.37), channel_id=1, source_target_pairs={{0,4},{4,0},{8,12},{12,8},{16,20},{20,16},{24,28},{28,24},{1,5},{5... | collective-permute-start | bytes 6152 | tf_op jit(solution)/shard_map/ppermute | solution.py:306
  18.8 5.0 %collective-permute-done = bf16[512,640]{1,0:T(8,128)(2,1)} collective-permute-done((bf16[512,640]{1,0:T(8,128)(2,1)}, bf16[512,640]{1,0:T(8,128)(2,1)}, u32[]{:S(2)}, u32[]{:S(2)}) %collective-permute-start) | collective-permute-done | bytes 655392 | tf_op jit(solution)/shard_map/ppermute | solution.py:306
  25.1 3.5 %collective-permute-start.4 = (bf16[512,640]{1,0:T(8,128)(2,1)S(1)}, bf16[512,640]{1,0:T(8,128)(2,1)S(1)}, u32[]{:S(2)}, u32[]{:S(2)}) collective-permute-start(bf16[512,640]{1,0:T(8,128)(2,1)S(1)} %get-tuple-element.56), channel_id=1, source_target_pairs={{0,8},{4,12},{8,16},{12,20},{16,24},{20,28},{1,9},{5,13},{9,17},{1... | collective-permute-start | bytes 1966088 | tf_op jit(solution)/shard_map/ppermute | solution.py:309
  32.5 3.8 %collective-permute-done.3 = bf16[512,640]{1,0:T(8,128)(2,1)S(1)} collective-permute-done((bf16[512,640]{1,0:T(8,128)(2,1)}, bf16[512,640]{1,0:T(8,128)(2,1)S(1)}, u32[]{:S(2)}, u32[]{:S(2)}) %collective-permute-start.3) | collective-permute-done | bytes 655392 | tf_op jit(solution)/shard_map/ppermute | solution.py:306
  36.5 3.4 %collective-permute-done.4.kp_ref = bf16[512,640]{1,0:T(8,128)(2,1)S(1)} collective-permute-done((bf16[512,640]{1,0:T(8,128)(2,1)S(1)}, bf16[512,640]{1,0:T(8,128)(2,1)S(1)}, u32[]{:S(2)}, u32[]{:S(2)}) %collective-permute-start.4) | collective-permute-done | bytes 655392 | tf_op jit(solution)/shard_map/ppermute | solution.py:309
  42.5 7.3 %collective-permute-start.5 = (bf16[640,640]{1,0:T(8,128)(2,1)S(1)}, bf16[640,640]{1,0:T(8,128)(2,1)S(1)}, u32[]{:S(2)}, u32[]{:S(2)}) collective-permute-start(bf16[640,640]{1,0:T(8,128)(2,1)S(1)} %get-tuple-element.77), channel_id=1, source_target_pairs={{0,8},{4,12},{24,16},{28,20},{1,9},{5,13},{25,17},{29,21},{2,10},{... | collective-permute-start | bytes 2457608 | tf_op jit(solution)/shard_map/ppermute | solution.py:309
  53.8 11.5 %collective-permute-done.5 = bf16[640,640]{1,0:T(8,128)(2,1)S(1)} collective-permute-done((bf16[640,640]{1,0:T(8,128)(2,1)S(1)}, bf16[640,640]{1,0:T(8,128)(2,1)S(1)}, u32[]{:S(2)}, u32[]{:S(2)}) %collective-permute-start.5) | collective-permute-done | bytes 819232 | tf_op jit(solution)/shard_map/ppermute | solution.py:309
  69.3 4.7 %collective-permute-start.8 = (bf16[512,640]{1,0:T(8,128)(2,1)S(1)}, bf16[512,640]{1,0:T(8,128)(2,1)S(1)}, u32[]{:S(2)}, u32[]{:S(2)}) collective-permute-start(bf16[512,640]{1,0:T(8,128)(2,1)S(1)} %get-tuple-element.33), channel_id=1, source_target_pairs={{0,8},{4,12},{1,9},{5,13},{2,10},{6,14},{3,11},{7,15}} | collective-permute-start | bytes 1966088 | tf_op jit(solution)/shard_map/ppermute | solution.py:309
  73.9 4.0 %collective-permute-done.6 = bf16[320,640]{1,0:T(8,128)(2,1)S(1)} collective-permute-done((bf16[320,640]{1,0:T(8,128)(2,1)S(1)}, bf16[320,640]{1,0:T(8,128)(2,1)S(1)}, u32[]{:S(2)}, u32[]{:S(2)}) %collective-permute-start.6) | collective-permute-done | bytes 409632 | tf_op jit(solution)/shard_map/ppermute | solution.py:309
  78.0 8.8 %collective-permute-done.9 = bf16[320,640]{1,0:T(8,128)(2,1)S(1)} collective-permute-done((bf16[320,640]{1,0:T(8,128)(2,1)S(1)}, bf16[320,640]{1,0:T(8,128)(2,1)S(1)}, u32[]{:S(2)}, u32[]{:S(2)}) %collective-permute-start.9) | collective-permute-done | bytes 409632 | tf_op jit(solution)/shard_map/ppermute | solution.py:309
  89.8 5.1 %collective-permute-done.8 = bf16[512,640]{1,0:T(8,128)(2,1)S(1)} collective-permute-done((bf16[512,640]{1,0:T(8,128)(2,1)S(1)}, bf16[512,640]{1,0:T(8,128)(2,1)S(1)}, u32[]{:S(2)}, u32[]{:S(2)}) %collective-permute-start.8) | collective-permute-done | bytes 655392 | tf_op jit(solution)/shard_map/ppermute | solution.py:309
  95.0 7.2 %collective-permute-done.11 = bf16[320,640]{1,0:T(8,128)(2,1)S(1)} collective-permute-done((bf16[320,640]{1,0:T(8,128)(2,1)S(1)}, bf16[320,640]{1,0:T(8,128)(2,1)S(1)}, u32[]{:S(2)}, u32[]{:S(2)}) %collective-permute-start.11) | collective-permute-done | bytes 409632 | tf_op jit(solution)/shard_map/ppermute | solution.py:309
  102.4 8.1 %shard_map.92 = bf16[640,640]{1,0:T(8,128)(2,1)S(1)} custom-call(s32[1]{0:T(128)} %bitcast.5.active_ref, f32[640,640]{1,0:T(8,128)S(1)} %pad_maximum_fusion.grad_ref, bf16[640,640]{1,0:T(8,128)(2,1)S(1)} %bitcast_select_fusion.init_ref), custom_call_target="tpu_custom_call" | custom-call | flops 4718592000 | bytes 3276800 | tf_op jit(solution)/shard_map/pallas_call | solution.py:164
  112.9 8.8 %collective-permute-done.12 = bf16[320,640]{1,0:T(8,128)(2,1)S(1)} collective-permute-done((bf16[320,640]{1,0:T(8,128)(2,1)S(1)}, bf16[320,640]{1,0:T(8,128)(2,1)S(1)}, u32[]{:S(2)}, u32[]{:S(2)}) %collective-permute-start.12) | collective-permute-done | bytes 409632 | tf_op jit(solution)/shard_map/ppermute | solution.py:309
  121.8 4.4 %collective-permute-start.14 = (bf16[320,640]{1,0:T(8,128)(2,1)S(1)}, bf16[320,640]{1,0:T(8,128)(2,1)S(1)}, u32[]{:S(2)}, u32[]{:S(2)}) collective-permute-start(bf16[320,640]{1,0:T(8,128)(2,1)S(1)} %get-tuple-element.68), channel_id=1, source_target_pairs={{0,8},{4,12},{24,16},{28,20},{1,9},{5,13},{25,17},{29,21},{2,10},{... | collective-permute-start | bytes 1228808 | tf_op jit(solution)/shard_map/ppermute | solution.py:309
  130.4 3.1 %collective-permute-done.14 = bf16[320,640]{1,0:T(8,128)(2,1)S(1)} collective-permute-done((bf16[320,640]{1,0:T(8,128)(2,1)S(1)}, bf16[320,640]{1,0:T(8,128)(2,1)S(1)}, u32[]{:S(2)}, u32[]{:S(2)}) %collective-permute-start.14) | collective-permute-done | bytes 409632 | tf_op jit(solution)/shard_map/ppermute | solution.py:309
  136.3 14.3 %shard_map.93.att_ref = f32[1024,640]{1,0:T(8,128)S(1)} custom-call(s32[1]{0:T(128)} %bitcast.10.first_ref, bf16[1024,640]{1,0:T(8,128)(2,1)S(1)} %pad_maximum_fusion.1.q_ref, bf16[512,640]{1,0:T(8,128)(2,1)S(1)} %collective-permute-done.4.kp_ref, bf16[1024,640]{1,0:T(8,128)(2,1)S(1)} %pad_maximum_fusion.2.k_ref, ...), custom_call_target="tpu_custom_call" | custom-call | flops 1677721600 | bytes 7864320 | tf_op jit(solution)/shard_map/pallas_call | solution.py:112
  153.2 5.1 %collective-permute-done.20 = bf16[640,640]{1,0:T(8,128)(2,1)S(1)} collective-permute-done((bf16[640,640]{1,0:T(8,128)(2,1)S(1)}, bf16[640,640]{1,0:T(8,128)(2,1)S(1)}, u32[]{:S(2)}, u32[]{:S(2)}) %collective-permute-start.20) | collective-permute-done | bytes 819232 | tf_op jit(solution)/shard_map/ppermute | solution.py:309
  165.5 8.6 %collective-permute-done.25.refs_2_ = bf16[512,640]{1,0:T(8,128)(2,1)S(1)} collective-permute-done((bf16[512,640]{1,0:T(8,128)(2,1)S(1)}, bf16[512,640]{1,0:T(8,128)(2,1)S(1)}, u32[]{:S(2)}, u32[]{:S(2)}) %collective-permute-start.25) | collective-permute-done | bytes 655392 | tf_op jit(solution)/shard_map/ppermute | solution.py:441
  176.3 4.7 %copy-done.2 = bf16[5120,1280]{1,0:T(8,128)(2,1)S(1)} copy-done((bf16[5120,1280]{1,0:T(8,128)(2,1)S(1)}, bf16[5120,1280]{1,0:T(8,128)(2,1)}, u32[]{:S(2)}) %copy-start.2) | copy-done | bytes 13107224
  181.0 7.5 %shard_map.96.refs_4_ = f32[512,1280]{1,0:T(8,128)S(1)} custom-call(s32[2]{0:T(128)S(1)} %pad_add_fusion.1.spot_ref, bf16[5120,1280]{1,0:T(8,128)(2,1)S(1)} %copy-done.2, bf16[512,640]{1,0:T(8,128)(2,1)S(1)} %shard_map.95.refs_0_, bf16[512,640]{1,0:T(8,128)(2,1)} %collective-permute-done.24.refs_1_, bf16[512,640]{1,0:T(8,128)(2,1)S(1)} %collective-permute-done.25.refs_2_, ...), custom_call_target="tpu_custom_call" | custom-call | flops 3355443200 | bytes 14417920 | tf_op jit(solution)/shard_map/pallas_call | solution.py:252
  188.6 2.6 %collective-permute-done.23.refs_2_ = bf16[512,640]{1,0:T(8,128)(2,1)S(1)} collective-permute-done((bf16[512,640]{1,0:T(8,128)(2,1)S(1)}, bf16[512,640]{1,0:T(8,128)(2,1)S(1)}, u32[]{:S(2)}, u32[]{:S(2)}) %collective-permute-start.23) | collective-permute-done | bytes 655392 | tf_op jit(solution)/shard_map/ppermute | solution.py:441
  193.3 4.7 %copy-done.3 = bf16[5120,1280]{1,0:T(8,128)(2,1)S(1)} copy-done((bf16[5120,1280]{1,0:T(8,128)(2,1)S(1)}, bf16[5120,1280]{1,0:T(8,128)(2,1)}, u32[]{:S(2)}) %copy-start.3) | copy-done | bytes 13107224
  198.1 8.0 %shard_map.97 = bf16[512,1280]{1,0:T(8,128)(2,1)} custom-call(s32[2]{0:T(128)S(1)} %pad_add_fusion.spot_ref, bf16[5120,1280]{1,0:T(8,128)(2,1)S(1)} %copy-done.3, bf16[512,640]{1,0:T(8,128)(2,1)S(1)} %collective-permute-done.21.refs_0_, bf16[512,640]{1,0:T(8,128)(2,1)S(1)} %collective-permute-done.22.refs_1_, ...), custom_call_target="tpu_custom_call" | custom-call | flops 3355443200 | bytes 14417920 | tf_op jit(solution)/shard_map/pallas_call | solution.py:252
  (104 shorter events, 58.5 us)
Async XLA Ops:
  0.8 39.1 %collective-permute-start.2 = (f32[512]{0:T(512)S(1)}, f32[512]{0:T(512)S(1)}, u32[]{:S(2)}, u32[]{:S(2)}) collective-permute-start(f32[512]{0:T(512)S(1)} %bitcast.37), channel_id=1, source_target_pairs={{0,4},{4,0},{8,12},{12,8},{16,20},{20,16},{24,28},{28,24},{1,5},{5... | collective-permute-start | bytes 6152 | tf_op jit(solution)/shard_map/ppermute | solution.py:306
  5.8 18.0 %collective-permute-start = (bf16[512,640]{1,0:T(8,128)(2,1)}, bf16[512,640]{1,0:T(8,128)(2,1)}, u32[]{:S(2)}, u32[]{:S(2)}) collective-permute-start(bf16[512,640]{1,0:T(8,128)(2,1)} %constant_dynamic-slice_fusion.5), channel_id=1, source_target_pairs={{0,4},{4,0},{8,12},{12,8},{16,20},{20,16},{24,28},{28,24},{1,5},{5... | collective-permute-start | bytes 1966088 | tf_op jit(solution)/shard_map/ppermute | solution.py:306
  8.1 28.2 %collective-permute-start.3 = (bf16[512,640]{1,0:T(8,128)(2,1)}, bf16[512,640]{1,0:T(8,128)(2,1)S(1)}, u32[]{:S(2)}, u32[]{:S(2)}) collective-permute-start(bf16[512,640]{1,0:T(8,128)(2,1)} %get-tuple-element.61), channel_id=1, source_target_pairs={{0,4},{4,0},{8,12},{12,8},{16,20},{20,16},{24,28},{28,24},{1,5},{5... | collective-permute-start | bytes 1966088 | tf_op jit(solution)/shard_map/ppermute | solution.py:306
  25.1 14.8 %collective-permute-start.4 = (bf16[512,640]{1,0:T(8,128)(2,1)S(1)}, bf16[512,640]{1,0:T(8,128)(2,1)S(1)}, u32[]{:S(2)}, u32[]{:S(2)}) collective-permute-start(bf16[512,640]{1,0:T(8,128)(2,1)S(1)} %get-tuple-element.56), channel_id=1, source_target_pairs={{0,8},{4,12},{8,16},{12,20},{16,24},{20,28},{1,9},{5,13},{9,17},{1... | collective-permute-start | bytes 1966088 | tf_op jit(solution)/shard_map/ppermute | solution.py:309
  36.2 32.6 %collective-permute-start.1 = (bf16[512,640]{1,0:T(8,128)(2,1)S(1)}, bf16[512,640]{1,0:T(8,128)(2,1)S(1)}, u32[]{:S(2)}, u32[]{:S(2)}) collective-permute-start(bf16[512,640]{1,0:T(8,128)(2,1)S(1)} %constant_dynamic-slice_fusion.6), channel_id=1, source_target_pairs={{0,4},{4,0},{8,12},{12,8},{16,20},{20,16},{24,28},{28,24},{1,5},{5... | collective-permute-start | bytes 1966088 | tf_op jit(solution)/shard_map/ppermute | solution.py:306
  41.8 84.5 %collective-permute-start.15 = (bf16[512,640]{1,0:T(8,128)(2,1)S(1)}, bf16[512,640]{1,0:T(8,128)(2,1)S(1)}, u32[]{:S(2)}, u32[]{:S(2)}) collective-permute-start(bf16[512,640]{1,0:T(8,128)(2,1)S(1)} %get-tuple-element.33), channel_id=1, source_target_pairs={{8,16},{12,20},{16,24},{20,28},{9,17},{13,21},{17,25},{21,29},{10,... | collective-permute-start | bytes 1966088 | tf_op jit(solution)/shard_map/ppermute | solution.py:309
  42.5 22.9 %collective-permute-start.5 = (bf16[640,640]{1,0:T(8,128)(2,1)S(1)}, bf16[640,640]{1,0:T(8,128)(2,1)S(1)}, u32[]{:S(2)}, u32[]{:S(2)}) collective-permute-start(bf16[640,640]{1,0:T(8,128)(2,1)S(1)} %get-tuple-element.77), channel_id=1, source_target_pairs={{0,8},{4,12},{24,16},{28,20},{1,9},{5,13},{25,17},{29,21},{2,10},{... | collective-permute-start | bytes 2457608 | tf_op jit(solution)/shard_map/ppermute | solution.py:309
  65.5 12.5 %collective-permute-start.6 = (bf16[320,640]{1,0:T(8,128)(2,1)S(1)}, bf16[320,640]{1,0:T(8,128)(2,1)S(1)}, u32[]{:S(2)}, u32[]{:S(2)}) collective-permute-start(bf16[320,640]{1,0:T(8,128)(2,1)S(1)} %get-tuple-element.30), channel_id=1, source_target_pairs={{0,8},{4,12},{8,0},{12,4},{16,24},{20,28},{24,16},{28,20},{1,9},{5... | collective-permute-start | bytes 1228808 | tf_op jit(solution)/shard_map/ppermute | solution.py:309
  68.1 18.7 %collective-permute-start.9 = (bf16[320,640]{1,0:T(8,128)(2,1)S(1)}, bf16[320,640]{1,0:T(8,128)(2,1)S(1)}, u32[]{:S(2)}, u32[]{:S(2)}) collective-permute-start(bf16[320,640]{1,0:T(8,128)(2,1)S(1)} %get-tuple-element.34), channel_id=1, source_target_pairs={{0,8},{4,12},{8,0},{12,4},{16,24},{20,28},{24,16},{28,20},{1,9},{5... | collective-permute-start | bytes 1228808 | tf_op jit(solution)/shard_map/ppermute | solution.py:309
  68.2 21.5 %collective-permute-start.7 = (bf16[640,640]{1,0:T(8,128)(2,1)S(1)}, bf16[640,640]{1,0:T(8,128)(2,1)S(1)}, u32[]{:S(2)}, u32[]{:S(2)}) collective-permute-start(bf16[640,640]{1,0:T(8,128)(2,1)S(1)} %get-tuple-element.53), channel_id=1, source_target_pairs={{16,8},{20,12},{17,9},{21,13},{18,10},{22,14},{19,11},{23,15}} | collective-permute-start | bytes 2457608 | tf_op jit(solution)/shard_map/ppermute | solution.py:309
  69.3 25.6 %collective-permute-start.8 = (bf16[512,640]{1,0:T(8,128)(2,1)S(1)}, bf16[512,640]{1,0:T(8,128)(2,1)S(1)}, u32[]{:S(2)}, u32[]{:S(2)}) collective-permute-start(bf16[512,640]{1,0:T(8,128)(2,1)S(1)} %get-tuple-element.33), channel_id=1, source_target_pairs={{0,8},{4,12},{1,9},{5,13},{2,10},{6,14},{3,11},{7,15}} | collective-permute-start | bytes 1966088 | tf_op jit(solution)/shard_map/ppermute | solution.py:309
  87.0 15.2 %collective-permute-start.10 = (bf16[320,640]{1,0:T(8,128)(2,1)S(1)}, bf16[320,640]{1,0:T(8,128)(2,1)S(1)}, u32[]{:S(2)}, u32[]{:S(2)}) collective-permute-start(bf16[320,640]{1,0:T(8,128)(2,1)S(1)} %get-tuple-element.49), channel_id=1, source_target_pairs={{16,0},{20,4},{8,24},{12,28},{17,1},{21,5},{9,25},{13,29},{18,2},{... | collective-permute-start | bytes 1228808 | tf_op jit(solution)/shard_map/ppermute | solution.py:309
  88.3 13.8 %collective-permute-start.11 = (bf16[320,640]{1,0:T(8,128)(2,1)S(1)}, bf16[320,640]{1,0:T(8,128)(2,1)S(1)}, u32[]{:S(2)}, u32[]{:S(2)}) collective-permute-start(bf16[320,640]{1,0:T(8,128)(2,1)S(1)} %get-tuple-element.57), channel_id=1, source_target_pairs={{16,0},{20,4},{8,24},{12,28},{17,1},{21,5},{9,25},{13,29},{18,2},{... | collective-permute-start | bytes 1228808 | tf_op jit(solution)/shard_map/ppermute | solution.py:309
  110.5 11.2 %collective-permute-start.12 = (bf16[320,640]{1,0:T(8,128)(2,1)S(1)}, bf16[320,640]{1,0:T(8,128)(2,1)S(1)}, u32[]{:S(2)}, u32[]{:S(2)}) collective-permute-start(bf16[320,640]{1,0:T(8,128)(2,1)S(1)} %slice.28), channel_id=1, source_target_pairs={{0,8},{4,12},{24,16},{28,20},{1,9},{5,13},{25,17},{29,21},{2,10},{... | collective-permute-start | bytes 1228808 | tf_op jit(solution)/shard_map/ppermute | solution.py:309
  111.9 18.3 %collective-permute-start.19 = (bf16[640,640]{1,0:T(8,128)(2,1)S(1)}, bf16[640,640]{1,0:T(8,128)(2,1)S(1)}, u32[]{:S(2)}, u32[]{:S(2)}) collective-permute-start(bf16[640,640]{1,0:T(8,128)(2,1)S(1)} %shard_map.91), channel_id=1, source_target_pairs={{8,16},{12,20},{9,17},{13,21},{10,18},{14,22},{11,19},{15,23}} | collective-permute-start | bytes 2457608 | tf_op jit(solution)/shard_map/ppermute | solution.py:309
  121.8 11.6 %collective-permute-start.14 = (bf16[320,640]{1,0:T(8,128)(2,1)S(1)}, bf16[320,640]{1,0:T(8,128)(2,1)S(1)}, u32[]{:S(2)}, u32[]{:S(2)}) collective-permute-start(bf16[320,640]{1,0:T(8,128)(2,1)S(1)} %get-tuple-element.68), channel_id=1, source_target_pairs={{0,8},{4,12},{24,16},{28,20},{1,9},{5,13},{25,17},{29,21},{2,10},{... | collective-permute-start | bytes 1228808 | tf_op jit(solution)/shard_map/ppermute | solution.py:309
  126.3 24.3 %collective-permute-start.13 = (bf16[320,640]{1,0:T(8,128)(2,1)S(1)}, bf16[320,640]{1,0:T(8,128)(2,1)S(1)}, u32[]{:S(2)}, u32[]{:S(2)}) collective-permute-start(bf16[320,640]{1,0:T(8,128)(2,1)S(1)} %slice.28), channel_id=1, source_target_pairs={{0,16},{4,20},{24,8},{28,12},{1,17},{5,21},{25,9},{29,13},{2,18},{... | collective-permute-start | bytes 1228808 | tf_op jit(solution)/shard_map/ppermute | solution.py:309
  127.6 23.0 %collective-permute-start.17 = (bf16[320,640]{1,0:T(8,128)(2,1)S(1)}, bf16[320,640]{1,0:T(8,128)(2,1)S(1)}, u32[]{:S(2)}, u32[]{:S(2)}) collective-permute-start(bf16[320,640]{1,0:T(8,128)(2,1)S(1)} %get-tuple-element.68), channel_id=1, source_target_pairs={{0,16},{4,20},{24,8},{28,12},{1,17},{5,21},{25,9},{29,13},{2,18},{... | collective-permute-start | bytes 1228808 | tf_op jit(solution)/shard_map/ppermute | solution.py:309
  129.0 21.6 %collective-permute-start.16 = (bf16[320,640]{1,0:T(8,128)(2,1)S(1)}, bf16[320,640]{1,0:T(8,128)(2,1)S(1)}, u32[]{:S(2)}, u32[]{:S(2)}) collective-permute-start(bf16[320,640]{1,0:T(8,128)(2,1)S(1)} %collective-permute-done.12), channel_id=1, source_target_pairs={{8,24},{12,28},{16,0},{20,4},{9,25},{13,29},{17,1},{21,5},{10,26},... | collective-permute-start | bytes 1228808 | tf_op jit(solution)/shard_map/ppermute | solution.py:309
  133.5 24.8 %collective-permute-start.20 = (bf16[640,640]{1,0:T(8,128)(2,1)S(1)}, bf16[640,640]{1,0:T(8,128)(2,1)S(1)}, u32[]{:S(2)}, u32[]{:S(2)}) collective-permute-start(bf16[640,640]{1,0:T(8,128)(2,1)S(1)} %broadcast_select_fusion), channel_id=1, source_target_pairs={{8,0},{12,4},{16,24},{20,28},{9,1},{13,5},{17,25},{21,29},{10,2},{... | collective-permute-start | bytes 2457608 | tf_op jit(solution)/shard_map/ppermute | solution.py:309
  134.8 18.1 %collective-permute-start.18 = (bf16[320,640]{1,0:T(8,128)(2,1)S(1)}, bf16[320,640]{1,0:T(8,128)(2,1)S(1)}, u32[]{:S(2)}, u32[]{:S(2)}) collective-permute-start(bf16[320,640]{1,0:T(8,128)(2,1)S(1)} %collective-permute-done.14), channel_id=1, source_target_pairs={{8,24},{12,28},{16,0},{20,4},{9,25},{13,29},{17,1},{21,5},{10,26},... | collective-permute-start | bytes 1228808 | tf_op jit(solution)/shard_map/ppermute | solution.py:309
  165.5 10.7 %collective-permute-start.24 = (bf16[512,640]{1,0:T(8,128)(2,1)S(1)}, bf16[512,640]{1,0:T(8,128)(2,1)}, u32[]{:S(2)}, u32[]{:S(2)}) collective-permute-start(bf16[512,640]{1,0:T(8,128)(2,1)S(1)} %shard_map.95.refs_0_), channel_id=1, source_target_pairs={{0,1},{1,0},{2,3},{3,2},{4,5},{5,4},{6,7},{7,6},{8,9},{9,8},{10,11... | collective-permute-start | bytes 1966088 | tf_op jit(solution)/shard_map/ppermute | solution.py:441
  175.6 15.6 %collective-permute-start.23 = (bf16[512,640]{1,0:T(8,128)(2,1)S(1)}, bf16[512,640]{1,0:T(8,128)(2,1)S(1)}, u32[]{:S(2)}, u32[]{:S(2)}) collective-permute-start(bf16[512,640]{1,0:T(8,128)(2,1)S(1)} %collective-permute-done.21.refs_0_), channel_id=1, source_target_pairs={{0,2},{1,3},{2,0},{3,1},{4,6},{5,7},{6,4},{7,5},{8,10},{9,11},{10,... | collective-permute-start | bytes 1966088 | tf_op jit(solution)/shard_map/ppermute | solution.py:441
  176.2 15.1 %collective-permute-start.22 = (bf16[512,640]{1,0:T(8,128)(2,1)S(1)}, bf16[512,640]{1,0:T(8,128)(2,1)S(1)}, u32[]{:S(2)}, u32[]{:S(2)}) collective-permute-start(bf16[512,640]{1,0:T(8,128)(2,1)S(1)} %collective-permute-done.21.refs_0_), channel_id=1, source_target_pairs={{0,1},{1,0},{2,3},{3,2},{4,5},{5,4},{6,7},{7,6},{8,9},{9,8},{10,11... | collective-permute-start | bytes 1966088 | tf_op jit(solution)/shard_map/ppermute | solution.py:441
  (13 other events, 63.9 us)

commit v2 on v1

--- a/solution.py
+++ b/solution.py
@@ -13,7 +13,7 @@
 NS_ITERS = 3
 PIECES = 2
 VMEM_BYTES = 24 * 1024 * 1024
-PROJECT_BYTES = 32 * 1024 * 1024
+PROJECT_BYTES = 52 * 1024 * 1024
 
 quintic_first = 3.4445
 quintic_second = -4.775
@@ -216,15 +216,15 @@
     )(jnp.reshape(which, (1,)).astype(jnp.int32), q, gate, lift, down, attended, gain)
 
 
-def project_kernel(offsets, group, has_total, spot_ref, w_ref, *refs):
-    count = len(offsets)
+def project_kernel(origins, group, has_total, spot_ref, w_ref, *refs):
+    count = len(origins)
     chunk_refs = refs[:count]
     total_ref = refs[count] if has_total else None
     out_ref, sum_ref, w_rows, arrived = refs[-4:]
     depth = w_rows.shape[1]
     copies = []
-    for number, offset in enumerate(offsets):
-        start = ((spot_ref[0] ^ offset) * group + spot_ref[1]) * depth
+    for number, (offset, head) in enumerate(origins):
+        start = ((spot_ref[0] ^ offset) * group + spot_ref[1 + head]) * depth
         copy = pltpu.make_async_copy(
             w_ref.at[pl.ds(pl.multiple_of(start, depth), depth)], w_rows.at[number], arrived.at[number]
         )
@@ -243,14 +243,15 @@
             sum_ref[...] = part
 
 
-def project(chunks, offsets, group, spot, weight, total, is_last):
+def project(parts, group, spot, weight, total, is_last):
+    chunks, origins = [part[0] for part in parts], [part[1:] for part in parts]
     count = len(chunks)
     rows, depth = chunks[0].shape
     columns = weight.shape[1]
     vmem = pl.BlockSpec(memory_space=pltpu.VMEM)
     operands = [spot, weight] + list(chunks) + ([] if total is None else [total])
     return pl.pallas_call(
-        functools.partial(project_kernel, offsets, group, total is not None),
+        functools.partial(project_kernel, origins, group, total is not None),
         out_shape=jax.ShapeDtypeStruct((rows, columns), bf16 if is_last else f32),
         in_specs=[pl.BlockSpec(memory_space=pltpu.SMEM), pl.BlockSpec(memory_space=pltpu.HBM)]
         + [vmem] * (len(operands) - 2),
@@ -312,6 +313,16 @@
             [(a * group + m, b * group + m) for a, b in pairs for m in range(group)],
         )
 
+    def by_side(array, pairs):
+        moves = []
+        for h in range(columns_of):
+            for a, b in pairs:
+                a, b = (a, b) if h % 2 == 0 else (planes - 1 - a, planes - 1 - b)
+                moves += [
+                    ((a * group + m) * columns_of + h, (b * group + m) * columns_of + h) for m in range(group)
+                ]
+        return lax.ppermute(array, ("ctx", "head"), moves)
+
     def head_columns(array, by):
         return lax.dynamic_slice_in_dim(array, (member + by) % group * width, width, 1)
 
@@ -333,8 +344,9 @@
         lax.dynamic_index_in_dim(learning_rates, (member + by) % group, 0, keepdims=False)
         for by in range(group)
     ]
+    sent_keys = keys[-1]
     keys = keys[:1] + [to_member(keys[by], by) for by in range(1, group)]
-    rates = rates[:1] + [to_member(rates[by], by) for by in range(1, group)]
+    rates = rates[:1] + [to_member(after(rates[by], sent_keys), by) for by in range(1, group)]
     values = values[:1] + [to_member(values[by], by) for by in range(1, group)]
     ordered_keys = in_order(keys)
     earlier_keys = between_planes(ordered_keys[-1][-WINDOW:], onward)
@@ -347,15 +359,14 @@
     total_down = 0.0
     for by in range(group):
         hidden, slope, silu = forwards[by]
-        block = values[by] if by < group - 1 else after(values[by], earlier_keys)
-        scaled = (rates[by][:, None] * block.astype(f32)).astype(bf16)
+        scaled = (rates[by][:, None] * values[by].astype(f32)).astype(bf16)
         total_down = total_down + mm(hidden, scaled, OVER_TOKENS)
         slopes.append(slope)
         silus.append(silu)
         scaleds.append(scaled)
     total_gate, total_lift = 0.0, 0.0
     for by in range(group):
-        scaled = scaleds[by] if by < group - 1 else after(scaleds[by], total_down)
+        scaled = scaleds[by] if by < group - 1 else after(scaleds[by], total_down, earlier_keys)
         backward = mm(scaled, down, ((1,), (1,)))
         total_gate = total_gate + mm(keys[by], (backward * slopes[by]).astype(bf16), OVER_TOKENS)
         total_lift = total_lift + mm(keys[by], (backward * silus[by]).astype(bf16), OVER_TOKENS)
@@ -373,20 +384,25 @@
         return own + between_planes(own.astype(bf16), pairs).astype(f32)
 
     down_levels = tree_mid(planes)
-    sum_down = add_from(total_down, down_levels[0])
+    side_plane = jnp.where(head_place % 2 == 0, plane, planes - 1 - plane)
+
+    def add_side(own, pairs):
+        return own + by_side(own.astype(bf16), pairs).astype(f32)
+
+    sum_down = add_side(total_down, down_levels[0])
     odd = plane % 2 == 1
     kept = cut(jnp.where(odd, total_lift, total_gate))
     given = cut(jnp.where(odd, total_gate, total_lift).astype(bf16))
     neighbours = [(i, i ^ 1) for i in range(planes)]
-    given = [between_planes(after(other, sum_down), neighbours) for other in given]
+    given = [between_planes(after(other, sum_down, values_early), neighbours) for other in given]
     first_sum = sum_down
     for level in down_levels[1:]:
-        sum_down = add_from(sum_down, level)
+        sum_down = add_side(sum_down, level)
     kept = [own + got.astype(f32) for own, got in zip(kept, given)]
     met = list(kept)
-    values_first = between_planes(after(window_values, first_sum), onward[:1])
+    values_first = between_planes(after(window_values, *met), onward[:1])
     earlier_values = jnp.where(plane == 1, values_first, values_early)
-    middle_plane = plane == planes // 2 - 1
+    middle_plane = side_plane == planes // 2 - 1
     new_down = renew(after(sum_down, values_first, *met), down, middle_plane)
     for level in tree_ends(planes):
         kept = [
@@ -407,7 +423,14 @@
     others = [pair for pair in swap if pair not in owners]
     is_owner_swap = functools.reduce(jnp.logical_or, [plane == b for _, b in owners])
     near, far = [], []
-    new_down = spread(new_down, [(b, a) for a, b in down_levels[-1]])
+    owned_down, owner = new_down, planes // 2 - 1
+    passed_on = []
+    for level in reversed(down_levels):
+        from_owner = [(b, a) for a, b in level if b == owner]
+        got = by_side(owned_down, from_owner)
+        here = functools.reduce(jnp.logical_or, [side_plane == b for _, b in from_owner])
+        new_down = jnp.where(here, got, new_down)
+        passed_on.append([(b, a) for a, b in level if b != owner])
     near, far = [], []
     for own in cut(new_outer):
         first = between_planes(own, owners)
@@ -420,8 +443,11 @@
         passed = passed if len(spread_halves(planes)) == 1 else own
         near.append(own)
         far.append((first, between_planes(passed, others)))
-    for level in reversed(down_levels[:-1]):
-        new_down = spread(after(new_down, *near), [(b, a) for a, b in level])
+    for pairs in passed_on:
+        if pairs:
+            got = by_side(after(new_down, near[0]), pairs)
+            here = functools.reduce(jnp.logical_or, [side_plane == b for _, b in pairs])
+            new_down = jnp.where(here, got, new_down)
 
     attended = attention(
         after(jnp.concatenate(in_order(asked)), *near),
@@ -448,20 +474,23 @@
             arrived.append((to_member(combined, group - by), (member + by) % group))
     arrived = [(combined, member)] + arrived
 
-    total = None
-    for number, (chunk, head) in enumerate(arrived):
-        parts = [chunk]
+    spot = jnp.stack([head_place] + [head for _, head in arrived]).astype(jnp.int32)
+
+    def widened(parts, bits):
         for bit in bits:
-            got = [swapped(part, bit) for part in parts]
-            if total is not None and bit == bits[0]:
-                got = [after(part, total) for part in got]
-            parts = [p for pair in zip(parts, got) for p in pair]
-        offsets = [0]
-        for bit in bits:
-            offsets = [p for o in offsets for p in (o, o ^ bit)]
-        spot = jnp.stack([head_place, head]).astype(jnp.int32)
-        total = project(parts, offsets, group, spot, output_weight, total, number == len(arrived) - 1)
-    return total
+            parts = [p for part, o, n in parts for p in ((part, o, n), (swapped(part, bit), o ^ bit, n))]
+        return parts
+
+    total, waiting = None, []
+    for number, (chunk, _) in enumerate(arrived):
+        waiting += widened([(chunk, 0, number)], bits[1:])
+        far = [(swapped(chunk, bits[0]), bits[0], number)]
+        if number == len(arrived) - 1:
+            total = project(waiting, group, spot, output_weight, total, False)
+            far = [(after(part, total), o, n) for part, o, n in far]
+            waiting = []
+        waiting += widened(far, bits[1:])
+    return project(waiting, group, spot, output_weight, total, True)
 
 
 def solution(mesh):

time: 207 us -> 208 us (level)
  waiting for transfers between devices: 82.8 us -> 66.9 us
  other arithmetic: 4.35 us -> 13.5 us
  matrix products: 15.4 us -> 21.5 us
  local copies, waits for them, and re-layouts: 16.9 us -> 11.1 us
  Pallas kernels: 43 us -> 47.4 us
    ppermute x17 -> x13, waiting for transfers between devices: 59.2 us -> 43.2 us  [between_planes(): lax.ppermute(array, 'ctx', [(a * group + m, b * group + m) for a, b in pa...]
    ppermute x17 -> x13, starting transfers between devices: 35.2 us -> 24.6 us  [between_planes(): lax.ppermute(array, 'ctx', [(a * group + m, b * group + m) for a, b in pa...]
    ppermute x0 -> x5, starting transfers between devices: none -> 10.1 us  [by_side(): return lax.ppermute(array, ('ctx', 'head'), moves)]
    ppermute x0 -> x5, waiting for transfers between devices: none -> 8.86 us  [by_side(): return lax.ppermute(array, ('ctx', 'head'), moves)]
    ppermute x5, waiting for transfers between devices: 10.2 us -> 2.44 us  [to_member(): return lax.ppermute(array, 'ctx', pairs)]
    unnamed x18 -> x60, local copies, waits for them, and re-layouts: 11.6 us -> 4.66 us
    dot_general x12, matrix products: 15.4 us -> 21.5 us  [mm(): return lax.dot_general(a, b, (dims, ((), ())), preferred_element_type=f32)]
    pallas_call x2, Pallas kernels: 15.5 us -> 19.9 us  [project(): pl.pallas_call(functools.partial(project_kernel, origins, group, total is...]
  transfers between devices with their start and end apart: 28 -> 29, of which waited for: 17 -> 13; matrix products, arithmetic and copies ran while one was open for 12% -> 19% of each run, Pallas kernels for 15% -> 17%
where the time goes in v2:
time: 208 us; the launch traced here: 206 us
  waiting for transfers between devices  66.9 us (32%)
  Pallas kernels  47.4 us (23%)
  starting transfers between devices  44.9 us (22%)
  matrix products  21.5 us (10%)
  other arithmetic  13.5 us (6%)
  local copies, waits for them, and re-layouts  11.1 us (5%)
    ppermute x13, waiting for transfers between devices, between_planes(): lax.ppermute(array, 'ctx', [(a * group + m, b * group + m) for a, b in pa...  43.2 us
    ppermute x13, starting transfers between devices, between_planes(): lax.ppermute(array, 'ctx', [(a * group + m, b * group + m) for a, b in pa...  24.6 us
    dot_general x12, matrix products, mm(): return lax.dot_general(a, b, (dims, ((), ())), preferred_element_type=f32)  21.5 us
    pallas_call x2, Pallas kernels, project(): pl.pallas_call(functools.partial(project_kernel, origins, group, total is...  19.9 us
    pallas_call x1, Pallas kernels, attention(): pl.pallas_call(attention_kernel, out_shape=jax.ShapeDtypeStruct((tokens,...  14.3 us
    ppermute x6, waiting for transfers between devices, swapped(): return lax.ppermute(part, 'head', [(i, i ^ bit) for i in range(columns_of)])  12.4 us
    ppermute x5, starting transfers between devices, by_side(): return lax.ppermute(array, ('ctx', 'head'), moves)  10.1 us
    ppermute x5, waiting for transfers between devices, by_side(): return lax.ppermute(array, ('ctx', 'head'), moves)  8.86 us
  transfers between devices with their start and end apart: 29, of which 13 were waited for; matrix products, arithmetic and copies ran while one was open for 19% of the time, Pallas kernels for 17%

profile of v2, /device:TPU:0, one launch (start us, length us, event | category | flops | bytes accessed | tf_op | source)
XLA Modules:
  0.0 206.0 jit_solution(17750287673464838740)
XLA Ops:
  2.1 3.0 %collective-permute-start = (bf16[512,640]{1,0:T(8,128)(2,1)}, bf16[512,640]{1,0:T(8,128)(2,1)}, u32[]{:S(2)}, u32[]{:S(2)}) collective-permute-start(bf16[512,640]{1,0:T(8,128)(2,1)} %constant_dynamic-slice_fusion.5), channel_id=1, source_target_pairs={{0,4},{4,0},{8,12},{12,8},{16,20},{20,16},{24,28},{28,24},{1,5},{5... | collective-permute-start | bytes 1966088 | tf_op jit(solution)/shard_map/ppermute | solution.py:307
  5.2 2.2 %constant_dynamic-slice_fusion.1 = (bf16[512,640]{1,0:T(8,128)(2,1)}, bf16[512,640]{1,0:T(8,128)(2,1)S(1)}) fusion(bf16[512,1280]{1,0:T(8,128)(2,1)} %param.11, s32[]{:T(128)S(6)} %select_n.203, s32[]{:T(128)S(6)} %select_n.211), kind=kLoop, calls=%fused_computation.73 | loop fusion | bytes 2621448 | tf_op jit(solution)/shard_map/dynamic_slice | solution.py:327
  20.5 2.9 %fusion.13 = f32[640,640]{1,0:T(8,128)S(1)} fusion(f32[512,640]{1,0:T(8,128)} %copy-done.19, f32[512,640]{1,0:T(8,128)} %copy-done.18, f32[512,640]{1,0:T(8,128)S(1)} %copy-done.17, bf16[512,1280]{1,0:T(8,128)(2,1)} %param.10, s32[]{:T(128)S(6)} %select_n.211), kind=kOutput, calls=%fused_computation.51 | convolution fusion | flops 422707200 | bytes 6225924 | tf_op jit(solution)/shard_map/dot_general | solution.py:27
  23.5 2.3 %broadcast_select_fusion.4 = (bf16[512,640]{1,0:T(8,128)(2,1)}, bf16[512,640]{1,0:T(8,128)(2,1)S(1)}) fusion(bf16[512,640]{1,0:T(8,128)(2,1)} %collective-permute-done, pred[]{:T(512)S(6)} %eq.74, bf16[512,1280]{1,0:T(8,128)(2,1)S(1)} %copy-done.4, s32[]{:T(128)S(6)} %select_n.211, pred[]{:T(512)S(6)} %eq.71), kind=kLoop, calls=%fused_computation.46 | loop fusion | flops 655360 | bytes 2621446 | tf_op jit(solution)/shard_map/jit(_where)/select_n | solution.py:37
  25.8 3.6 %collective-permute-start.4 = (bf16[512,640]{1,0:T(8,128)(2,1)S(1)}, bf16[512,640]{1,0:T(8,128)(2,1)S(1)}, u32[]{:S(2)}, u32[]{:S(2)}) collective-permute-start(bf16[512,640]{1,0:T(8,128)(2,1)S(1)} %get-tuple-element.56), channel_id=1, source_target_pairs={{0,8},{4,12},{8,16},{12,20},{16,24},{20,28},{1,9},{5,13},{9,17},{1... | collective-permute-start | bytes 1966088 | tf_op jit(solution)/shard_map/ppermute | solution.py:310
  39.0 6.7 %collective-permute-start.5 = (bf16[640,640]{1,0:T(8,128)(2,1)S(1)}, bf16[640,640]{1,0:T(8,128)(2,1)S(1)}, u32[]{:S(2)}, u32[]{:S(2)}) collective-permute-start(bf16[640,640]{1,0:T(8,128)(2,1)S(1)} %get-tuple-element.77), channel_id=1, source_target_pairs={{0,8},{4,12},{24,16},{28,20},{25,17},{29,21},{1,9},{5,13},{2,10},{... | collective-permute-start | bytes 2457608 | tf_op jit(solution)/shard_map/ppermute | solution.py:324
  48.5 3.7 %select_convert_fusion = (bf16[640,640]{1,0:T(8,128)(2,1)S(1)}, f32[640,640]{1,0:T(8,128)}) fusion(f32[640,640]{1,0:T(8,128)S(1)} %convolution_add_fusion.1, pred[]{:T(512)S(6)} %eq.70, f32[640,640]{1,0:T(8,128)S(1)} %fusion.13, bf16[512,640]{1,0:T(8,128)(2,1)} %collective-permute-done, f32[512,640]{1,0:T(8,128)S(1)} %fusion.42, ...), kind=kOutput, calls=%fused_computation.3 | convolution fusion | flops 423526400 | bytes 10321921 | tf_op jit(solution)/shard_map/dot_general | solution.py:27
  53.1 8.9 %collective-permute-done.5 = bf16[640,640]{1,0:T(8,128)(2,1)S(1)} collective-permute-done((bf16[640,640]{1,0:T(8,128)(2,1)S(1)}, bf16[640,640]{1,0:T(8,128)(2,1)S(1)}, u32[]{:S(2)}, u32[]{:S(2)}) %collective-permute-start.5) | collective-permute-done | bytes 819232 | tf_op jit(solution)/shard_map/ppermute | solution.py:324
  64.3 2.5 %collective-permute-start.7 = (bf16[320,640]{1,0:T(8,128)(2,1)}, bf16[320,640]{1,0:T(8,128)(2,1)}, u32[]{:S(2)}, u32[]{:S(2)}) collective-permute-start(bf16[320,640]{1,0:T(8,128)(2,1)} %get-tuple-element.32), channel_id=1, source_target_pairs={{0,8},{4,12},{8,0},{12,4},{16,24},{20,28},{24,16},{28,20},{1,9},{5... | collective-permute-start | bytes 1228808 | tf_op jit(solution)/shard_map/ppermute | solution.py:310
  71.7 5.8 %collective-permute-done.7 = bf16[320,640]{1,0:T(8,128)(2,1)} collective-permute-done((bf16[320,640]{1,0:T(8,128)(2,1)}, bf16[320,640]{1,0:T(8,128)(2,1)}, u32[]{:S(2)}, u32[]{:S(2)}) %collective-permute-start.7) | collective-permute-done | bytes 409632 | tf_op jit(solution)/shard_map/ppermute | solution.py:310
  77.5 5.8 %collective-permute-done.9 = bf16[320,640]{1,0:T(8,128)(2,1)} collective-permute-done((bf16[320,640]{1,0:T(8,128)(2,1)}, bf16[320,640]{1,0:T(8,128)(2,1)}, u32[]{:S(2)}, u32[]{:S(2)}) %collective-permute-start.9) | collective-permute-done | bytes 409632 | tf_op jit(solution)/shard_map/ppermute | solution.py:310
  84.6 3.9 %collective-permute-start.10 = (bf16[512,640]{1,0:T(8,128)(2,1)S(1)}, bf16[512,640]{1,0:T(8,128)(2,1)S(1)}, u32[]{:S(2)}, u32[]{:S(2)}) collective-permute-start(bf16[512,640]{1,0:T(8,128)(2,1)S(1)} %copy-done.10), channel_id=1, source_target_pairs={{0,8},{4,12},{1,9},{5,13},{2,10},{6,14},{3,11},{7,15}} | collective-permute-start | bytes 1966088 | tf_op jit(solution)/shard_map/ppermute | solution.py:310
  92.9 6.4 %collective-permute-done.10 = bf16[512,640]{1,0:T(8,128)(2,1)S(1)} collective-permute-done((bf16[512,640]{1,0:T(8,128)(2,1)S(1)}, bf16[512,640]{1,0:T(8,128)(2,1)S(1)}, u32[]{:S(2)}, u32[]{:S(2)}) %collective-permute-start.10) | collective-permute-done | bytes 655392 | tf_op jit(solution)/shard_map/ppermute | solution.py:310
  101.4 12.7 %collective-permute-done.12 = bf16[320,640]{1,0:T(8,128)(2,1)S(1)} collective-permute-done((bf16[320,640]{1,0:T(8,128)(2,1)S(1)}, bf16[320,640]{1,0:T(8,128)(2,1)S(1)}, u32[]{:S(2)}, u32[]{:S(2)}) %collective-permute-start.12) | collective-permute-done | bytes 409632 | tf_op jit(solution)/shard_map/ppermute | solution.py:310
  114.3 8.1 %shard_map.92 = bf16[640,640]{1,0:T(8,128)(2,1)S(1)} custom-call(s32[1]{0:T(128)} %bitcast.6.active_ref, f32[640,640]{1,0:T(8,128)S(1)} %pad_maximum_fusion.grad_ref, bf16[640,640]{1,0:T(8,128)(2,1)S(1)} %bitcast_select_fusion.init_ref), custom_call_target="tpu_custom_call" | custom-call | flops 4718592000 | bytes 3276800 | tf_op jit(solution)/shard_map/pallas_call | solution.py:164
  125.4 8.1 %collective-permute-done.13 = bf16[320,640]{1,0:T(8,128)(2,1)S(1)} collective-permute-done((bf16[320,640]{1,0:T(8,128)(2,1)S(1)}, bf16[320,640]{1,0:T(8,128)(2,1)S(1)}, u32[]{:S(2)}, u32[]{:S(2)}) %collective-permute-start.13) | collective-permute-done | bytes 409632 | tf_op jit(solution)/shard_map/ppermute | solution.py:310
  133.6 4.4 %collective-permute-start.15 = (bf16[320,640]{1,0:T(8,128)(2,1)S(1)}, bf16[320,640]{1,0:T(8,128)(2,1)S(1)}, u32[]{:S(2)}, u32[]{:S(2)}) collective-permute-start(bf16[320,640]{1,0:T(8,128)(2,1)S(1)} %get-tuple-element.68), channel_id=1, source_target_pairs={{0,8},{4,12},{24,16},{28,20},{1,9},{5,13},{25,17},{29,21},{2,10},{... | collective-permute-start | bytes 1228808 | tf_op jit(solution)/shard_map/ppermute | solution.py:310
  141.6 4.4 %collective-permute-done.15 = bf16[320,640]{1,0:T(8,128)(2,1)S(1)} collective-permute-done((bf16[320,640]{1,0:T(8,128)(2,1)S(1)}, bf16[320,640]{1,0:T(8,128)(2,1)S(1)}, u32[]{:S(2)}, u32[]{:S(2)}) %collective-permute-start.15) | collective-permute-done | bytes 409632 | tf_op jit(solution)/shard_map/ppermute | solution.py:310
  147.6 14.3 %shard_map.93.att_ref = f32[1024,640]{1,0:T(8,128)S(1)} custom-call(s32[1]{0:T(128)} %bitcast.11.first_ref, bf16[1024,640]{1,0:T(8,128)(2,1)S(1)} %pad_maximum_fusion.1.q_ref, bf16[512,640]{1,0:T(8,128)(2,1)S(1)} %collective-permute-done.4.kp_ref, bf16[1024,640]{1,0:T(8,128)(2,1)S(1)} %get-tuple-element.79.k_ref, ...), custom_call_target="tpu_custom_call" | custom-call | flops 1677721600 | bytes 7864320 | tf_op jit(solution)/shard_map/pallas_call | solution.py:112
  162.4 2.5 %shard_map.94 = bf16[512,640]{1,0:T(8,128)(2,1)S(1)} custom-call(s32[1]{0:T(128)} %bitcast.3.which_ref, bf16[512,640]{1,0:T(8,128)(2,1)S(1)} %collective-permute-done.1.q_ref, bf16[640,640]{1,0:T(8,128)(2,1)S(1)} %pad_maximum_fusion.4.gate_ref, bf16[640,640]{1,0:T(8,128)(2,1)S(1)} %pad_maximum_fusion.5.lift_ref, ...), custom_call_target="tpu_custom_call" | custom-call | flops 1258291200 | bytes 5734400 | tf_op jit(solution)/shard_map/pallas_call | solution.py:194
  164.9 2.5 %shard_map.95.refs_0_ = bf16[512,640]{1,0:T(8,128)(2,1)S(1)} custom-call(s32[1]{0:T(128)} %bitcast.12.which_ref, bf16[512,640]{1,0:T(8,128)(2,1)S(1)} %get-tuple-element.45.q_ref, bf16[640,640]{1,0:T(8,128)(2,1)S(1)} %pad_maximum_fusion.4.gate_ref, bf16[640,640]{1,0:T(8,128)(2,1)S(1)} %pad_maximum_fusion.5.lift_ref, ...), custom_call_target="tpu_custom_call" | custom-call | flops 1258291200 | bytes 5734400 | tf_op jit(solution)/shard_map/pallas_call | solution.py:194
  170.6 7.6 %collective-permute-done.25.refs_2_ = bf16[512,640]{1,0:T(8,128)(2,1)S(1)} collective-permute-done((bf16[512,640]{1,0:T(8,128)(2,1)S(1)}, bf16[512,640]{1,0:T(8,128)(2,1)S(1)}, u32[]{:S(2)}, u32[]{:S(2)}) %collective-permute-start.25) | collective-permute-done | bytes 655392 | tf_op jit(solution)/shard_map/ppermute | solution.py:467
  182.6 13.0 %shard_map.96.refs_2_ = f32[512,1280]{1,0:T(8,128)} custom-call(s32[3]{0:T(128)S(1)} %pad_add_fusion.spot_ref, bf16[5120,1280]{1,0:T(8,128)(2,1)} %w_ref.3, bf16[512,640]{1,0:T(8,128)(2,1)S(1)} %shard_map.95.refs_0_, bf16[512,640]{1,0:T(8,128)(2,1)S(1)} %collective-permute-done.24.refs_1_, bf16[512,640]{1,0:T(8,128)(2,1)S(1)} %collective-permute-done.25.refs_2_, ...), custom_call_target="tpu_custom_call" | custom-call | flops 5033164800 | bytes 19005440 | tf_op jit(solution)/shard_map/pallas_call | solution.py:253
  198.9 6.9 %shard_map.97 = bf16[512,1280]{1,0:T(8,128)(2,1)} custom-call(s32[3]{0:T(128)S(1)} %pad_add_fusion.spot_ref, bf16[5120,1280]{1,0:T(8,128)(2,1)} %w_ref.3, bf16[512,640]{1,0:T(8,128)(2,1)S(1)} %collective-permute-done.23.refs_0_, bf16[512,640]{1,0:T(8,128)(2,1)S(1)} %collective-permute-done.28.refs_1_, f32[512,1280]{1,0:T(8,128)} %shard_map.96.refs_2_), custom_call_target="tpu_custom_call" | custom-call | flops 1677721600 | bytes 9830400 | tf_op jit(solution)/shard_map/pallas_call | solution.py:253
  (147 shorter events, 63.0 us)
Async XLA Ops:
  2.1 21.3 %collective-permute-start = (bf16[512,640]{1,0:T(8,128)(2,1)}, bf16[512,640]{1,0:T(8,128)(2,1)}, u32[]{:S(2)}, u32[]{:S(2)}) collective-permute-start(bf16[512,640]{1,0:T(8,128)(2,1)} %constant_dynamic-slice_fusion.5), channel_id=1, source_target_pairs={{0,4},{4,0},{8,12},{12,8},{16,20},{20,16},{24,28},{28,24},{1,5},{5... | collective-permute-start | bytes 1966088 | tf_op jit(solution)/shard_map/ppermute | solution.py:307
  5.1 29.1 %collective-permute-start.2 = (f32[512]{0:T(512)S(1)}, f32[512]{0:T(512)S(1)}, u32[]{:S(2)}, u32[]{:S(2)}) collective-permute-start(f32[512]{0:T(512)S(1)} %bitcast.37), channel_id=1, source_target_pairs={{0,4},{4,0},{8,12},{12,8},{16,20},{20,16},{24,28},{28,24},{1,5},{5... | collective-permute-start | bytes 6152 | tf_op jit(solution)/shard_map/ppermute | solution.py:307
  7.4 26.8 %collective-permute-start.3 = (bf16[512,640]{1,0:T(8,128)(2,1)}, bf16[512,640]{1,0:T(8,128)(2,1)}, u32[]{:S(2)}, u32[]{:S(2)}) collective-permute-start(bf16[512,640]{1,0:T(8,128)(2,1)} %get-tuple-element.61), channel_id=1, source_target_pairs={{0,4},{4,0},{8,12},{12,8},{16,20},{20,16},{24,28},{28,24},{1,5},{5... | collective-permute-start | bytes 1966088 | tf_op jit(solution)/shard_map/ppermute | solution.py:307
  25.8 19.9 %collective-permute-start.4 = (bf16[512,640]{1,0:T(8,128)(2,1)S(1)}, bf16[512,640]{1,0:T(8,128)(2,1)S(1)}, u32[]{:S(2)}, u32[]{:S(2)}) collective-permute-start(bf16[512,640]{1,0:T(8,128)(2,1)S(1)} %get-tuple-element.56), channel_id=1, source_target_pairs={{0,8},{4,12},{8,16},{12,20},{16,24},{20,28},{1,9},{5,13},{9,17},{1... | collective-permute-start | bytes 1966088 | tf_op jit(solution)/shard_map/ppermute | solution.py:310
  38.3 25.1 %collective-permute-start.6 = (bf16[512,640]{1,0:T(8,128)(2,1)S(1)}, bf16[512,640]{1,0:T(8,128)(2,1)S(1)}, u32[]{:S(2)}, u32[]{:S(2)}) collective-permute-start(bf16[512,640]{1,0:T(8,128)(2,1)S(1)} %get-tuple-element.34), channel_id=1, source_target_pairs={{8,16},{12,20},{16,24},{20,28},{9,17},{13,21},{17,25},{21,29},{10,... | collective-permute-start | bytes 1966088 | tf_op jit(solution)/shard_map/ppermute | solution.py:310
  39.0 23.0 %collective-permute-start.5 = (bf16[640,640]{1,0:T(8,128)(2,1)S(1)}, bf16[640,640]{1,0:T(8,128)(2,1)S(1)}, u32[]{:S(2)}, u32[]{:S(2)}) collective-permute-start(bf16[640,640]{1,0:T(8,128)(2,1)S(1)} %get-tuple-element.77), channel_id=1, source_target_pairs={{0,8},{4,12},{24,16},{28,20},{25,17},{29,21},{1,9},{5,13},{2,10},{... | collective-permute-start | bytes 2457608 | tf_op jit(solution)/shard_map/ppermute | solution.py:324
  64.3 13.2 %collective-permute-start.7 = (bf16[320,640]{1,0:T(8,128)(2,1)}, bf16[320,640]{1,0:T(8,128)(2,1)}, u32[]{:S(2)}, u32[]{:S(2)}) collective-permute-start(bf16[320,640]{1,0:T(8,128)(2,1)} %get-tuple-element.32), channel_id=1, source_target_pairs={{0,8},{4,12},{8,0},{12,4},{16,24},{20,28},{24,16},{28,20},{1,9},{5... | collective-permute-start | bytes 1228808 | tf_op jit(solution)/shard_map/ppermute | solution.py:310
  66.8 16.5 %collective-permute-start.9 = (bf16[320,640]{1,0:T(8,128)(2,1)}, bf16[320,640]{1,0:T(8,128)(2,1)}, u32[]{:S(2)}, u32[]{:S(2)}) collective-permute-start(bf16[320,640]{1,0:T(8,128)(2,1)} %get-tuple-element.33), channel_id=1, source_target_pairs={{0,8},{4,12},{8,0},{12,4},{16,24},{20,28},{24,16},{28,20},{1,9},{5... | collective-permute-start | bytes 1228808 | tf_op jit(solution)/shard_map/ppermute | solution.py:310
  67.8 21.0 %collective-permute-start.1 = (bf16[512,640]{1,0:T(8,128)(2,1)}, bf16[512,640]{1,0:T(8,128)(2,1)S(1)}, u32[]{:S(2)}, u32[]{:S(2)}) collective-permute-start(bf16[512,640]{1,0:T(8,128)(2,1)} %constant_dynamic-slice_fusion.6), channel_id=1, source_target_pairs={{0,4},{4,0},{8,12},{12,8},{16,20},{20,16},{24,28},{28,24},{1,5},{5... | collective-permute-start | bytes 1966088 | tf_op jit(solution)/shard_map/ppermute | solution.py:307
  69.3 23.4 %collective-permute-start.8 = (bf16[640,640]{1,0:T(8,128)(2,1)S(1)}, bf16[640,640]{1,0:T(8,128)(2,1)S(1)}, u32[]{:S(2)}, u32[]{:S(2)}) collective-permute-start(bf16[640,640]{1,0:T(8,128)(2,1)S(1)} %get-tuple-element.53), channel_id=1, source_target_pairs={{16,8},{20,12},{9,17},{13,21},{18,10},{22,14},{11,19},{15,23}} | collective-permute-start | bytes 2457608 | tf_op jit(solution)/shard_map/ppermute | solution.py:324
  84.6 14.6 %collective-permute-start.10 = (bf16[512,640]{1,0:T(8,128)(2,1)S(1)}, bf16[512,640]{1,0:T(8,128)(2,1)S(1)}, u32[]{:S(2)}, u32[]{:S(2)}) collective-permute-start(bf16[512,640]{1,0:T(8,128)(2,1)S(1)} %copy-done.10), channel_id=1, source_target_pairs={{0,8},{4,12},{1,9},{5,13},{2,10},{6,14},{3,11},{7,15}} | collective-permute-start | bytes 1966088 | tf_op jit(solution)/shard_map/ppermute | solution.py:310
  90.1 24.0 %collective-permute-start.11 = (bf16[320,640]{1,0:T(8,128)(2,1)S(1)}, bf16[320,640]{1,0:T(8,128)(2,1)S(1)}, u32[]{:S(2)}, u32[]{:S(2)}) collective-permute-start(bf16[320,640]{1,0:T(8,128)(2,1)S(1)} %get-tuple-element.49), channel_id=1, source_target_pairs={{16,0},{20,4},{8,24},{12,28},{17,1},{21,5},{9,25},{13,29},{18,2},{... | collective-permute-start | bytes 1228808 | tf_op jit(solution)/shard_map/ppermute | solution.py:310
  91.4 22.7 %collective-permute-start.12 = (bf16[320,640]{1,0:T(8,128)(2,1)S(1)}, bf16[320,640]{1,0:T(8,128)(2,1)S(1)}, u32[]{:S(2)}, u32[]{:S(2)}) collective-permute-start(bf16[320,640]{1,0:T(8,128)(2,1)S(1)} %get-tuple-element.57), channel_id=1, source_target_pairs={{16,0},{20,4},{8,24},{12,28},{17,1},{21,5},{9,25},{13,29},{18,2},{... | collective-permute-start | bytes 1228808 | tf_op jit(solution)/shard_map/ppermute | solution.py:310
  99.3 40.1 %collective-permute-start.20 = (bf16[640,640]{1,0:T(8,128)(2,1)S(1)}, bf16[640,640]{1,0:T(8,128)(2,1)S(1)}, u32[]{:S(2)}, u32[]{:S(2)}) collective-permute-start(bf16[640,640]{1,0:T(8,128)(2,1)S(1)} %shard_map.91), channel_id=1, source_target_pairs={{8,16},{12,20},{17,9},{21,13},{10,18},{14,22},{19,11},{23,15}} | collective-permute-start | bytes 2457608 | tf_op jit(solution)/shard_map/ppermute | solution.py:324
  100.1 40.7 %collective-permute-start.19 = (bf16[640,640]{1,0:T(8,128)(2,1)S(1)}, bf16[640,640]{1,0:T(8,128)(2,1)S(1)}, u32[]{:S(2)}, u32[]{:S(2)}) collective-permute-start(bf16[640,640]{1,0:T(8,128)(2,1)S(1)} %shard_map.91), channel_id=1, source_target_pairs={{8,0},{12,4},{17,25},{21,29},{10,2},{14,6},{19,27},{23,31}} | collective-permute-start | bytes 2457608 | tf_op jit(solution)/shard_map/ppermute | solution.py:324
  122.4 11.1 %collective-permute-start.13 = (bf16[320,640]{1,0:T(8,128)(2,1)S(1)}, bf16[320,640]{1,0:T(8,128)(2,1)S(1)}, u32[]{:S(2)}, u32[]{:S(2)}) collective-permute-start(bf16[320,640]{1,0:T(8,128)(2,1)S(1)} %slice.28), channel_id=1, source_target_pairs={{0,8},{4,12},{24,16},{28,20},{1,9},{5,13},{25,17},{29,21},{2,10},{... | collective-permute-start | bytes 1228808 | tf_op jit(solution)/shard_map/ppermute | solution.py:310
  124.0 37.9 %collective-permute-start.14 = (bf16[320,640]{1,0:T(8,128)(2,1)S(1)}, bf16[320,640]{1,0:T(8,128)(2,1)S(1)}, u32[]{:S(2)}, u32[]{:S(2)}) collective-permute-start(bf16[320,640]{1,0:T(8,128)(2,1)S(1)} %slice.28), channel_id=1, source_target_pairs={{0,16},{4,20},{24,8},{28,12},{1,17},{5,21},{25,9},{29,13},{2,18},{... | collective-permute-start | bytes 1228808 | tf_op jit(solution)/shard_map/ppermute | solution.py:310
  133.6 12.4 %collective-permute-start.15 = (bf16[320,640]{1,0:T(8,128)(2,1)S(1)}, bf16[320,640]{1,0:T(8,128)(2,1)S(1)}, u32[]{:S(2)}, u32[]{:S(2)}) collective-permute-start(bf16[320,640]{1,0:T(8,128)(2,1)S(1)} %get-tuple-element.68), channel_id=1, source_target_pairs={{0,8},{4,12},{24,16},{28,20},{1,9},{5,13},{25,17},{29,21},{2,10},{... | collective-permute-start | bytes 1228808 | tf_op jit(solution)/shard_map/ppermute | solution.py:310
  138.1 23.7 %collective-permute-start.17 = (bf16[320,640]{1,0:T(8,128)(2,1)S(1)}, bf16[320,640]{1,0:T(8,128)(2,1)S(1)}, u32[]{:S(2)}, u32[]{:S(2)}) collective-permute-start(bf16[320,640]{1,0:T(8,128)(2,1)S(1)} %get-tuple-element.68), channel_id=1, source_target_pairs={{0,16},{4,20},{24,8},{28,12},{1,17},{5,21},{25,9},{29,13},{2,18},{... | collective-permute-start | bytes 1228808 | tf_op jit(solution)/shard_map/ppermute | solution.py:310
  139.5 22.4 %collective-permute-start.16 = (bf16[320,640]{1,0:T(8,128)(2,1)S(1)}, bf16[320,640]{1,0:T(8,128)(2,1)S(1)}, u32[]{:S(2)}, u32[]{:S(2)}) collective-permute-start(bf16[320,640]{1,0:T(8,128)(2,1)S(1)} %collective-permute-done.13), channel_id=1, source_target_pairs={{8,24},{12,28},{16,0},{20,4},{9,25},{13,29},{17,1},{21,5},{10,26},... | collective-permute-start | bytes 1228808 | tf_op jit(solution)/shard_map/ppermute | solution.py:310
  140.9 21.4 %collective-permute-start.21 = (bf16[640,640]{1,0:T(8,128)(2,1)S(1)}, bf16[640,640]{1,0:T(8,128)(2,1)S(1)}, u32[]{:S(2)}, u32[]{:S(2)}) collective-permute-start(bf16[640,640]{1,0:T(8,128)(2,1)S(1)} %select_select_fusion), channel_id=1, source_target_pairs={{16,24},{20,28},{9,1},{13,5},{18,26},{22,30},{11,3},{15,7}} | collective-permute-start | bytes 2457608 | tf_op jit(solution)/shard_map/ppermute | solution.py:324
  146.1 15.9 %collective-permute-start.18 = (bf16[320,640]{1,0:T(8,128)(2,1)S(1)}, bf16[320,640]{1,0:T(8,128)(2,1)S(1)}, u32[]{:S(2)}, u32[]{:S(2)}) collective-permute-start(bf16[320,640]{1,0:T(8,128)(2,1)S(1)} %collective-permute-done.15), channel_id=1, source_target_pairs={{8,24},{12,28},{16,0},{20,4},{9,25},{13,29},{17,1},{21,5},{10,26},... | collective-permute-start | bytes 1228808 | tf_op jit(solution)/shard_map/ppermute | solution.py:310
  167.5 10.7 %collective-permute-start.25 = (bf16[512,640]{1,0:T(8,128)(2,1)S(1)}, bf16[512,640]{1,0:T(8,128)(2,1)S(1)}, u32[]{:S(2)}, u32[]{:S(2)}) collective-permute-start(bf16[512,640]{1,0:T(8,128)(2,1)S(1)} %shard_map.95.refs_0_), channel_id=1, source_target_pairs={{0,2},{1,3},{2,0},{3,1},{4,6},{5,7},{6,4},{7,5},{8,10},{9,11},{10,... | collective-permute-start | bytes 1966088 | tf_op jit(solution)/shard_map/ppermute | solution.py:467
  179.7 17.1 %collective-permute-start.23 = (bf16[512,640]{1,0:T(8,128)(2,1)S(1)}, bf16[512,640]{1,0:T(8,128)(2,1)S(1)}, u32[]{:S(2)}, u32[]{:S(2)}) collective-permute-start(bf16[512,640]{1,0:T(8,128)(2,1)S(1)} %collective-permute-done.22.refs_4_), channel_id=1, source_target_pairs={{0,2},{1,3},{2,0},{3,1},{4,6},{5,7},{6,4},{7,5},{8,10},{9,11},{10,... | collective-permute-start | bytes 1966088 | tf_op jit(solution)/shard_map/ppermute | solution.py:467
  (35 other events, 210.2 us)

commit v3 on v2

--- a/solution.py
+++ b/solution.py
@@ -12,8 +12,8 @@
 WINDOW = 512
 NS_ITERS = 3
 PIECES = 2
-VMEM_BYTES = 24 * 1024 * 1024
-PROJECT_BYTES = 52 * 1024 * 1024
+VMEM_BYTES = 20 * 1024 * 1024
+PROJECT_BYTES = 28 * 1024 * 1024
 
 quintic_first = 3.4445
 quintic_second = -4.775
@@ -73,36 +73,48 @@
     return levels + [[(middle, middle - 1)]]
 
 
-def spread_halves(count):
-    half = count // 2
-    low = [[(b, a) for a, b in level] for level in reversed(tree_low(0, half))]
-    return [level + [(count - 1 - a, count - 1 - b) for a, b in level] for level in low]
-
-
-def attention_kernel(first_ref, q_ref, kp_ref, k_ref, vp_ref, v_ref, out_ref, k_all, v_all):
+def spread_ends(count):
+    levels, step = [], count // 2
+    while step > 1:
+        low = [(i, i + step) for i in range(0, count, 2 * step)]
+        levels.append(low + [(count - 1 - a, count - 1 - b) for a, b in low])
+        step //= 2
+    return levels
+
+
+def attention_kernel(first_ref, q_ref, kp_ref, k_ref, vp_ref, v_ref, out_ref, k_all, v_turned):
     tokens = q_ref.shape[0]
     tile = ATT_HD
     span = WINDOW + tile
     k_all[:WINDOW] = kp_ref[...]
     k_all[WINDOW:] = k_ref[...]
-    v_all[:WINDOW] = vp_ref[...]
-    v_all[WINDOW:] = v_ref[...]
+    v_turned[:, :WINDOW] = vp_ref[...].T
+    v_turned[:, WINDOW:] = v_ref[...].T
     is_first = first_ref[0] == 0
-    row = lax.broadcasted_iota(jnp.int32, (tile, span), 0)
-    col = lax.broadcasted_iota(jnp.int32, (tile, span), 1)
-    allowed = (col > row) & (col <= row + WINDOW)
+    key = lax.broadcasted_iota(jnp.int32, (tile, tile), 0)
+    query = lax.broadcasted_iota(jnp.int32, (tile, tile), 1)
     scale = ATT_HD**-0.5 * math.log2(math.e)
     for number in range(tokens // tile):
         start = number * tile
-        s = mm(q_ref[start : start + tile], k_all[start : start + span], ((1,), (1,))) * scale
-        keep = allowed
+        s = mm(k_all[start : start + span], q_ref[start : start + tile], ((1,), (1,)))
+        inner = s[tile:WINDOW]
+        head_rows = key > query
         if start < WINDOW:
-            keep = keep & ((col >= WINDOW - start) | jnp.logical_not(is_first))
-        s = jnp.where(keep, s, -1e30)
-        w = jnp.exp2(s - jnp.max(s, axis=1, keepdims=True))
-        total = jnp.sum(w, axis=1, keepdims=True)
-        o = mm(w.astype(bf16), v_all[start : start + span])
-        out_ref[start : start + tile] = o / total
+            head_rows = head_rows & jnp.logical_not(is_first)
+            place = start + tile + lax.broadcasted_iota(jnp.int32, inner.shape, 0)
+            inner = jnp.where((place >= WINDOW) | jnp.logical_not(is_first), inner, -1e30)
+        s = jnp.concatenate(
+            [
+                jnp.where(head_rows, s[:tile], -1e30),
+                inner,
+                jnp.where(key <= query, s[WINDOW:], -1e30),
+            ]
+        )
+        peak = jnp.max(s, axis=0, keepdims=True)
+        w = jnp.exp2((s - peak) * scale)
+        total = jnp.sum(w, axis=0, keepdims=True)
+        o = mm(v_turned[:, start : start + span], w.astype(bf16))
+        out_ref[start : start + tile] = (o / total).T
 
 
 def attention(q, kp, k, vp, v, plane):
@@ -117,7 +129,10 @@
             grid=(width // ATT_HD,),
             in_specs=[wide, before, wide, before, wide],
             out_specs=wide,
-            scratch_shapes=[pltpu.VMEM((WINDOW + tokens, ATT_HD), bf16)] * 2,
+            scratch_shapes=[
+                pltpu.VMEM((WINDOW + tokens, ATT_HD), bf16),
+                pltpu.VMEM((ATT_HD, WINDOW + tokens), bf16),
+            ],
         ),
         compiler_params=pltpu.CompilerParams(vmem_limit_bytes=VMEM_BYTES),
         cost_estimate=pl.CostEstimate(
@@ -263,7 +278,7 @@
         ],
         compiler_params=pltpu.CompilerParams(vmem_limit_bytes=PROJECT_BYTES),
         cost_estimate=pl.CostEstimate(
-            flops=2 * count * rows * depth * columns,
+            flops=16 * count * rows * depth * columns,
             bytes_accessed=2 * count * (rows + columns) * depth + 8 * rows * columns,
             transcendentals=0,
         ),
@@ -352,7 +367,6 @@
     earlier_keys = between_planes(ordered_keys[-1][-WINDOW:], onward)
     forwards = [forward(block, gate, lift) for block in keys]
     hidden = forwards[-1][0]
-    asked = asked[:1] + [to_member(after(asked[by], hidden), by) for by in range(1, group)]
     values = values[:1] + [after(block, hidden) for block in values[1:]]
 
     hiddens, slopes, silus, scaleds = [], [], [], []
@@ -390,6 +404,7 @@
         return own + by_side(own.astype(bf16), pairs).astype(f32)
 
     sum_down = add_side(total_down, down_levels[0])
+    asked = asked[:1] + [to_member(after(asked[by], sum_down), by) for by in range(1, group)]
     odd = plane % 2 == 1
     kept = cut(jnp.where(odd, total_lift, total_gate))
     given = cut(jnp.where(odd, total_gate, total_lift).astype(bf16))
@@ -400,7 +415,7 @@
         sum_down = add_side(sum_down, level)
     kept = [own + got.astype(f32) for own, got in zip(kept, given)]
     met = list(kept)
-    values_first = between_planes(after(window_values, *met), onward[:1])
+    values_first = between_planes(after(window_values, first_sum), onward[:1])
     earlier_values = jnp.where(plane == 1, values_first, values_early)
     middle_plane = side_plane == planes // 2 - 1
     new_down = renew(after(sum_down, values_first, *met), down, middle_plane)
@@ -417,13 +432,7 @@
     low_plane, high_plane = plane == 0, plane == planes - 1
     new_sums = jnp.concatenate(kept)
     new_outer = renew(after(new_sums, new_down), jnp.where(low_plane, gate, lift), low_plane | high_plane)
-    half = planes // 2
-    swap = [(i, (i + half) % planes) for i in range(planes)]
-    owners = [pair for pair in swap if pair[0] in (0, planes - 1)]
-    others = [pair for pair in swap if pair not in owners]
-    is_owner_swap = functools.reduce(jnp.logical_or, [plane == b for _, b in owners])
-    near, far = [], []
-    owned_down, owner = new_down, planes // 2 - 1
+    owned_down, owner = after(new_down, new_sums), planes // 2 - 1
     passed_on = []
     for level in reversed(down_levels):
         from_owner = [(b, a) for a, b in level if b == owner]
@@ -431,18 +440,22 @@
         here = functools.reduce(jnp.logical_or, [side_plane == b for _, b in from_owner])
         new_down = jnp.where(here, got, new_down)
         passed_on.append([(b, a) for a, b in level if b != owner])
-    near, far = [], []
+    far_levels = spread_ends(planes)
+    from_ends = [(i, i ^ 1) for i in (0, planes - 1)]
+    from_others = [(i, i ^ 1) for i in range(1, planes - 1)]
+    near, passed_by = [], []
     for own in cut(new_outer):
-        first = between_planes(own, owners)
         passed = own
-        for level in spread_halves(planes):
+        for level in far_levels:
             got = between_planes(own, level)
             here = functools.reduce(jnp.logical_or, [plane == b for _, b in level])
             own = jnp.where(here, got, own)
             passed = got
-        passed = passed if len(spread_halves(planes)) == 1 else own
         near.append(own)
-        far.append((first, between_planes(passed, others)))
+        passed_by.append(passed if len(far_levels) == 1 else own)
+    other_ends = between_planes(after(new_outer, passed_by[0]), from_ends)
+    others = jnp.concatenate([between_planes(passed, from_others) for passed in passed_by])
+    beside_end = (plane == 1) | (plane == planes - 2)
     for pairs in passed_on:
         if pairs:
             got = by_side(after(new_down, near[0]), pairs)
@@ -457,10 +470,10 @@
         jnp.concatenate(ordered_values),
         plane,
     )
-    lower = plane < half
-    far = [jnp.where(is_owner_swap, after(first, attended), after(other, attended)) for first, other in far]
-    new_gate = jnp.concatenate([jnp.where(lower, a, b) for a, b in zip(near, far)])
-    new_lift = jnp.concatenate([jnp.where(lower, b, a) for a, b in zip(near, far)])
+    other = jnp.where(beside_end, after(other_ends, attended), after(others, attended))
+    mine, even = jnp.concatenate(near), plane % 2 == 0
+    new_gate, new_lift = jnp.where(even, mine, other), jnp.where(even, other, mine)
+
     bits = [1 << k for k in reversed(range(columns_of.bit_length() - 1))]
 
     def swapped(part, bit):

time: 208 us -> 194 us (0.933)
  Pallas kernels: 47.4 us -> 35.8 us
  waiting for transfers between devices: 66.9 us -> 76.8 us
  other arithmetic: 13.5 us -> 7.99 us
  local copies, waits for them, and re-layouts: 11.1 us -> 7.45 us
    pallas_call x1, Pallas kernels: 14.3 us -> 7.62 us  [attention(): pl.pallas_call(attention_kernel, out_shape=jax.ShapeDtypeStruct((tokens,...]
    ppermute x6, waiting for transfers between devices: 12.4 us -> 18.4 us  [swapped(): return lax.ppermute(part, 'head', [(i, i ^ bit) for i in range(columns_of)])]
    pallas_call x2, Pallas kernels: 19.9 us -> 15.1 us  [project(): pl.pallas_call(functools.partial(project_kernel, origins, group, total is...]
    unnamed x60 -> x40, local copies, waits for them, and re-layouts: 4.66 us -> 1.51 us
    ppermute x5, waiting for transfers between devices: 8.86 us -> 11.4 us  [by_side(): return lax.ppermute(array, ('ctx', 'head'), moves)]
    ppermute x13 -> x12, waiting for transfers between devices: 43.2 us -> 44.5 us  [between_planes(): lax.ppermute(array, 'ctx', [(a * group + m, b * group + m) for a, b in pa...]
    ppermute x13 -> x12, starting transfers between devices: 24.6 us -> 24.3 us  [between_planes(): lax.ppermute(array, 'ctx', [(a * group + m, b * group + m) for a, b in pa...]
  transfers between devices with their start and end apart: 29 -> 28, of which waited for: 13 -> 15; matrix products, arithmetic and copies ran while one was open for 19% -> 16% of each run, Pallas kernels for 17% -> 14%
where the time goes in v3:
time: 194 us; the launch traced here: 193 us
  waiting for transfers between devices  76.8 us (40%)
  starting transfers between devices  45.1 us (23%)
  Pallas kernels  35.8 us (18%)
  matrix products  19.5 us (10%)
  other arithmetic  7.99 us (4%)
  local copies, waits for them, and re-layouts  7.45 us (4%)
    ppermute x12, waiting for transfers between devices, between_planes(): lax.ppermute(array, 'ctx', [(a * group + m, b * group + m) for a, b in pa...  44.5 us
    ppermute x12, starting transfers between devices, between_planes(): lax.ppermute(array, 'ctx', [(a * group + m, b * group + m) for a, b in pa...  24.3 us
    dot_general x12, matrix products, mm(): return lax.dot_general(a, b, (dims, ((), ())), preferred_element_type=f32)  19.5 us
    ppermute x6, waiting for transfers between devices, swapped(): return lax.ppermute(part, 'head', [(i, i ^ bit) for i in range(columns_of)])  18.4 us
    pallas_call x2, Pallas kernels, project(): pl.pallas_call(functools.partial(project_kernel, origins, group, total is...  15.1 us
    ppermute x5, waiting for transfers between devices, by_side(): return lax.ppermute(array, ('ctx', 'head'), moves)  11.4 us
    ppermute x5, starting transfers between devices, by_side(): return lax.ppermute(array, ('ctx', 'head'), moves)  10.3 us
    pallas_call x2, Pallas kernels, renew(): pl.pallas_call(settle_kernel, out_shape=jax.ShapeDtypeStruct((rows, colum...  8.14 us
  transfers between devices with their start and end apart: 28, of which 15 were waited for; matrix products, arithmetic and copies ran while one was open for 16% of the time, Pallas kernels for 14%

profile of v3, /device:TPU:0, one launch (start us, length us, event | category | flops | bytes accessed | tf_op | source)
XLA Modules:
  0.0 193.5 jit_solution(18004325148007518897)
XLA Ops:
  2.1 3.0 %collective-permute-start = (bf16[512,640]{1,0:T(8,128)(2,1)}, bf16[512,640]{1,0:T(8,128)(2,1)}, u32[]{:S(2)}, u32[]{:S(2)}) collective-permute-start(bf16[512,640]{1,0:T(8,128)(2,1)} %constant_dynamic-slice_fusion.3), channel_id=1, source_target_pairs={{0,4},{4,0},{8,12},{12,8},{16,20},{20,16},{24,28},{28,24},{1,5},{5... | collective-permute-start | bytes 1966088 | tf_op jit(solution)/shard_map/ppermute | solution.py:322
  5.2 2.3 %constant_dynamic-slice_fusion.1 = (bf16[512,640]{1,0:T(8,128)(2,1)}, bf16[512,640]{1,0:T(8,128)(2,1)S(1)}) fusion(bf16[512,1280]{1,0:T(8,128)(2,1)} %param.11, s32[]{:T(128)S(6)} %select_n.195, s32[]{:T(128)S(6)} %select_n.197), kind=kLoop, calls=%fused_computation.70 | loop fusion | bytes 2621448 | tf_op jit(solution)/shard_map/dynamic_slice | solution.py:342
  21.5 2.6 %fusion.13 = f32[640,640]{1,0:T(8,128)S(1)} fusion(f32[512,640]{1,0:T(8,128)} %copy-done.11, f32[512,640]{1,0:T(8,128)} %copy-done.10, f32[512,640]{1,0:T(8,128)S(1)} %copy-done.9, bf16[512,1280]{1,0:T(8,128)(2,1)S(1)} %copy-done.3, s32[]{:T(128)S(6)} %select_n.197), kind=kOutput, calls=%fused_computation.54 | convolution fusion | flops 422707200 | bytes 6225924 | tf_op jit(solution)/shard_map/dot_general | solution.py:27
  25.4 3.6 %collective-permute-start.5 = (bf16[512,640]{1,0:T(8,128)(2,1)S(1)}, bf16[512,640]{1,0:T(8,128)(2,1)S(1)}, u32[]{:S(2)}, u32[]{:S(2)}) collective-permute-start(bf16[512,640]{1,0:T(8,128)(2,1)S(1)} %get-tuple-element.58), channel_id=1, source_target_pairs={{0,8},{4,12},{8,16},{12,20},{16,24},{20,28},{1,9},{5,13},{9,17},{1... | collective-permute-start | bytes 1966088 | tf_op jit(solution)/shard_map/ppermute | solution.py:325
  38.2 6.7 %collective-permute-start.3 = (bf16[640,640]{1,0:T(8,128)(2,1)S(1)}, bf16[640,640]{1,0:T(8,128)(2,1)S(1)}, u32[]{:S(2)}, u32[]{:S(2)}) collective-permute-start(bf16[640,640]{1,0:T(8,128)(2,1)S(1)} %get-tuple-element.73), channel_id=1, source_target_pairs={{0,8},{4,12},{24,16},{28,20},{25,17},{29,21},{1,9},{5,13},{2,10},{... | collective-permute-start | bytes 2457608 | tf_op jit(solution)/shard_map/ppermute | solution.py:339
  49.8 11.4 %collective-permute-done.3 = bf16[640,640]{1,0:T(8,128)(2,1)S(1)} collective-permute-done((bf16[640,640]{1,0:T(8,128)(2,1)S(1)}, bf16[640,640]{1,0:T(8,128)(2,1)S(1)}, u32[]{:S(2)}, u32[]{:S(2)}) %collective-permute-start.3) | collective-permute-done | bytes 819232 | tf_op jit(solution)/shard_map/ppermute | solution.py:339
  61.4 2.5 %collective-permute-start.7 = (bf16[320,640]{1,0:T(8,128)(2,1)S(1)}, bf16[320,640]{1,0:T(8,128)(2,1)S(1)}, u32[]{:S(2)}, u32[]{:S(2)}) collective-permute-start(bf16[320,640]{1,0:T(8,128)(2,1)S(1)} %get-tuple-element.32), channel_id=1, source_target_pairs={{0,8},{4,12},{8,0},{12,4},{16,24},{20,28},{24,16},{28,20},{1,9},{5... | collective-permute-start | bytes 1228808 | tf_op jit(solution)/shard_map/ppermute | solution.py:325
  64.4 3.9 %collective-permute-start.9 = (bf16[512,640]{1,0:T(8,128)(2,1)S(1)}, bf16[512,640]{1,0:T(8,128)(2,1)S(1)}, u32[]{:S(2)}, u32[]{:S(2)}) collective-permute-start(bf16[512,640]{1,0:T(8,128)(2,1)S(1)} %get-tuple-element.33), channel_id=1, source_target_pairs={{0,8},{4,12},{1,9},{5,13},{2,10},{6,14},{3,11},{7,15}} | collective-permute-start | bytes 1966088 | tf_op jit(solution)/shard_map/ppermute | solution.py:325
  70.9 3.4 %collective-permute-done.7 = bf16[320,640]{1,0:T(8,128)(2,1)S(1)} collective-permute-done((bf16[320,640]{1,0:T(8,128)(2,1)S(1)}, bf16[320,640]{1,0:T(8,128)(2,1)S(1)}, u32[]{:S(2)}, u32[]{:S(2)}) %collective-permute-start.7) | collective-permute-done | bytes 409632 | tf_op jit(solution)/shard_map/ppermute | solution.py:325
  74.4 8.3 %collective-permute-done.10 = bf16[320,640]{1,0:T(8,128)(2,1)S(1)} collective-permute-done((bf16[320,640]{1,0:T(8,128)(2,1)S(1)}, bf16[320,640]{1,0:T(8,128)(2,1)S(1)}, u32[]{:S(2)}, u32[]{:S(2)}) %collective-permute-start.10) | collective-permute-done | bytes 409632 | tf_op jit(solution)/shard_map/ppermute | solution.py:325
  85.5 8.0 %collective-permute-done.9 = bf16[512,640]{1,0:T(8,128)(2,1)S(1)} collective-permute-done((bf16[512,640]{1,0:T(8,128)(2,1)S(1)}, bf16[512,640]{1,0:T(8,128)(2,1)S(1)}, u32[]{:S(2)}, u32[]{:S(2)}) %collective-permute-start.9) | collective-permute-done | bytes 655392 | tf_op jit(solution)/shard_map/ppermute | solution.py:325
  93.8 7.9 %collective-permute-done.12 = bf16[320,640]{1,0:T(8,128)(2,1)S(1)} collective-permute-done((bf16[320,640]{1,0:T(8,128)(2,1)S(1)}, bf16[320,640]{1,0:T(8,128)(2,1)S(1)}, u32[]{:S(2)}, u32[]{:S(2)}) %collective-permute-start.12) | collective-permute-done | bytes 409632 | tf_op jit(solution)/shard_map/ppermute | solution.py:325
  104.0 8.1 %shard_map.92 = bf16[640,640]{1,0:T(8,128)(2,1)S(1)} custom-call(s32[1]{0:T(128)} %bitcast.8.active_ref, f32[640,640]{1,0:T(8,128)S(1)} %pad_maximum_fusion.grad_ref, bf16[640,640]{1,0:T(8,128)(2,1)S(1)} %bitcast_select_fusion.init_ref), custom_call_target="tpu_custom_call" | custom-call | flops 4718592000 | bytes 3276800 | tf_op jit(solution)/shard_map/pallas_call | solution.py:179
  113.8 8.6 %collective-permute-done.13 = bf16[320,640]{1,0:T(8,128)(2,1)S(1)} collective-permute-done((bf16[320,640]{1,0:T(8,128)(2,1)S(1)}, bf16[320,640]{1,0:T(8,128)(2,1)S(1)}, u32[]{:S(2)}, u32[]{:S(2)}) %collective-permute-start.13) | collective-permute-done | bytes 409632 | tf_op jit(solution)/shard_map/ppermute | solution.py:325
  122.5 5.4 %collective-permute-start.14 = (bf16[320,640]{1,0:T(8,128)(2,1)S(1)}, bf16[320,640]{1,0:T(8,128)(2,1)S(1)}, u32[]{:S(2)}, u32[]{:S(2)}) collective-permute-start(bf16[320,640]{1,0:T(8,128)(2,1)S(1)} %get-tuple-element.66), channel_id=1, source_target_pairs={{0,16},{4,20},{24,8},{28,12},{1,17},{5,21},{25,9},{29,13},{2,18},{... | collective-permute-start | bytes 1228808 | tf_op jit(solution)/shard_map/ppermute | solution.py:325
  131.6 4.9 %collective-permute-done.14 = bf16[320,640]{1,0:T(8,128)(2,1)S(1)} collective-permute-done((bf16[320,640]{1,0:T(8,128)(2,1)S(1)}, bf16[320,640]{1,0:T(8,128)(2,1)S(1)}, u32[]{:S(2)}, u32[]{:S(2)}) %collective-permute-start.14) | collective-permute-done | bytes 409632 | tf_op jit(solution)/shard_map/ppermute | solution.py:325
  138.1 7.6 %shard_map.93.att_ref = f32[1024,640]{1,0:T(8,128)S(1)} custom-call(s32[1]{0:T(128)} %bitcast.11.first_ref, bf16[1024,640]{1,0:T(8,128)(2,1)S(1)} %pad_maximum_fusion.1.q_ref, bf16[512,640]{1,0:T(8,128)(2,1)S(1)} %collective-permute-done.5.kp_ref, bf16[1024,640]{1,0:T(8,128)(2,1)S(1)} %get-tuple-element.77.k_ref, ...), custom_call_target="tpu_custom_call" | custom-call | flops 1677721600 | bytes 7864320 | tf_op jit(solution)/shard_map/pallas_call | solution.py:124
  145.7 3.3 %collective-permute-done.17 = bf16[320,640]{1,0:T(8,128)(2,1)S(1)} collective-permute-done((bf16[320,640]{1,0:T(8,128)(2,1)S(1)}, bf16[320,640]{1,0:T(8,128)(2,1)S(1)}, u32[]{:S(2)}, u32[]{:S(2)}) %collective-permute-start.17) | collective-permute-done | bytes 409632 | tf_op jit(solution)/shard_map/ppermute | solution.py:325
  149.7 2.5 %shard_map.94 = bf16[512,640]{1,0:T(8,128)(2,1)S(1)} custom-call(s32[1]{0:T(128)} %bitcast.3.which_ref, bf16[512,640]{1,0:T(8,128)(2,1)S(1)} %collective-permute-done.4.q_ref, bf16[640,640]{1,0:T(8,128)(2,1)S(1)} %get-tuple-element.56.gate_ref, bf16[640,640]{1,0:T(8,128)(2,1)S(1)} %get-tuple-element.55.lift_ref, ...), custom_call_target="tpu_custom_call" | custom-call | flops 1258291200 | bytes 5734400 | tf_op jit(solution)/shard_map/pallas_call | solution.py:209
  152.2 2.5 %shard_map.95.refs_0_ = bf16[512,640]{1,0:T(8,128)(2,1)S(1)} custom-call(s32[1]{0:T(128)} %bitcast.12.which_ref, bf16[512,640]{1,0:T(8,128)(2,1)S(1)} %get-tuple-element.45.q_ref, bf16[640,640]{1,0:T(8,128)(2,1)S(1)} %get-tuple-element.56.gate_ref, bf16[640,640]{1,0:T(8,128)(2,1)S(1)} %get-tuple-element.55.lift_ref, ...), custom_call_target="tpu_custom_call" | custom-call | flops 1258291200 | bytes 5734400 | tf_op jit(solution)/shard_map/pallas_call | solution.py:209
  157.8 10.4 %collective-permute-done.24.refs_2_ = bf16[512,640]{1,0:T(8,128)(2,1)S(1)} collective-permute-done((bf16[512,640]{1,0:T(8,128)(2,1)S(1)}, bf16[512,640]{1,0:T(8,128)(2,1)S(1)}, u32[]{:S(2)}, u32[]{:S(2)}) %collective-permute-start.24) | collective-permute-done | bytes 655392 | tf_op jit(solution)/shard_map/ppermute | solution.py:480
  171.4 10.4 %shard_map.96.refs_2_ = f32[512,1280]{1,0:T(8,128)S(1)} custom-call(s32[3]{0:T(128)S(1)} %pad_add_fusion.spot_ref, bf16[5120,1280]{1,0:T(8,128)(2,1)S(1)} %bitcast.36, bf16[512,640]{1,0:T(8,128)(2,1)S(1)} %shard_map.95.refs_0_, bf16[512,640]{1,0:T(8,128)(2,1)S(1)} %collective-permute-done.23.refs_1_, bf16[512,640]{1,0:T(8,128)(2,1)S(1)} %collective-permute-done.24.refs_2_, ...), custom_call_target="tpu_custom_call" | custom-call | flops 40265318400 | bytes 19005440 | tf_op jit(solution)/shard_map/pallas_call | solution.py:268
  181.9 4.7 %collective-permute-done.22.refs_0_ = bf16[512,640]{1,0:T(8,128)(2,1)S(1)} collective-permute-done((bf16[512,640]{1,0:T(8,128)(2,1)S(1)}, bf16[512,640]{1,0:T(8,128)(2,1)S(1)}, u32[]{:S(2)}, u32[]{:S(2)}) %collective-permute-start.22) | collective-permute-done | bytes 655392 | tf_op jit(solution)/shard_map/ppermute | solution.py:480
  188.6 4.6 %shard_map.97 = bf16[512,1280]{1,0:T(8,128)(2,1)} custom-call(s32[3]{0:T(128)S(1)} %pad_add_fusion.spot_ref, bf16[5120,1280]{1,0:T(8,128)(2,1)S(1)} %bitcast.36, bf16[512,640]{1,0:T(8,128)(2,1)S(1)} %collective-permute-done.22.refs_0_, bf16[512,640]{1,0:T(8,128)(2,1)S(1)} %collective-permute-done.27.refs_1_, f32[512,1280]{1,0:T(8,128)S(1)} %shard_map.96.refs_2_), custom_call_target="tpu_custom_call" | custom-call | flops 13421772800 | bytes 9830400 | tf_op jit(solution)/shard_map/pallas_call | solution.py:268
  (124 shorter events, 55.9 us)
Async XLA Ops:
  2.1 21.9 %collective-permute-start = (bf16[512,640]{1,0:T(8,128)(2,1)}, bf16[512,640]{1,0:T(8,128)(2,1)}, u32[]{:S(2)}, u32[]{:S(2)}) collective-permute-start(bf16[512,640]{1,0:T(8,128)(2,1)} %constant_dynamic-slice_fusion.3), channel_id=1, source_target_pairs={{0,4},{4,0},{8,12},{12,8},{16,20},{20,16},{24,28},{28,24},{1,5},{5... | collective-permute-start | bytes 1966088 | tf_op jit(solution)/shard_map/ppermute | solution.py:322
  5.1 29.1 %collective-permute-start.1 = (f32[512]{0:T(512)S(1)}, f32[512]{0:T(512)S(1)}, u32[]{:S(2)}, u32[]{:S(2)}) collective-permute-start(f32[512]{0:T(512)S(1)} %bitcast.39), channel_id=1, source_target_pairs={{0,4},{4,0},{8,12},{12,8},{16,20},{20,16},{24,28},{28,24},{1,5},{5... | collective-permute-start | bytes 6152 | tf_op jit(solution)/shard_map/ppermute | solution.py:322
  7.5 26.7 %collective-permute-start.2 = (bf16[512,640]{1,0:T(8,128)(2,1)}, bf16[512,640]{1,0:T(8,128)(2,1)}, u32[]{:S(2)}, u32[]{:S(2)}) collective-permute-start(bf16[512,640]{1,0:T(8,128)(2,1)} %get-tuple-element.63), channel_id=1, source_target_pairs={{0,4},{4,0},{8,12},{12,8},{16,20},{20,16},{24,28},{28,24},{1,5},{5... | collective-permute-start | bytes 1966088 | tf_op jit(solution)/shard_map/ppermute | solution.py:322
  25.4 19.5 %collective-permute-start.5 = (bf16[512,640]{1,0:T(8,128)(2,1)S(1)}, bf16[512,640]{1,0:T(8,128)(2,1)S(1)}, u32[]{:S(2)}, u32[]{:S(2)}) collective-permute-start(bf16[512,640]{1,0:T(8,128)(2,1)S(1)} %get-tuple-element.58), channel_id=1, source_target_pairs={{0,8},{4,12},{8,16},{12,20},{16,24},{20,28},{1,9},{5,13},{9,17},{1... | collective-permute-start | bytes 1966088 | tf_op jit(solution)/shard_map/ppermute | solution.py:325
  37.5 24.0 %collective-permute-start.6 = (bf16[512,640]{1,0:T(8,128)(2,1)S(1)}, bf16[512,640]{1,0:T(8,128)(2,1)S(1)}, u32[]{:S(2)}, u32[]{:S(2)}) collective-permute-start(bf16[512,640]{1,0:T(8,128)(2,1)S(1)} %get-tuple-element.33), channel_id=1, source_target_pairs={{8,16},{12,20},{16,24},{20,28},{9,17},{13,21},{17,25},{21,29},{10,... | collective-permute-start | bytes 1966088 | tf_op jit(solution)/shard_map/ppermute | solution.py:325
  38.2 23.0 %collective-permute-start.3 = (bf16[640,640]{1,0:T(8,128)(2,1)S(1)}, bf16[640,640]{1,0:T(8,128)(2,1)S(1)}, u32[]{:S(2)}, u32[]{:S(2)}) collective-permute-start(bf16[640,640]{1,0:T(8,128)(2,1)S(1)} %get-tuple-element.73), channel_id=1, source_target_pairs={{0,8},{4,12},{24,16},{28,20},{25,17},{29,21},{1,9},{5,13},{2,10},{... | collective-permute-start | bytes 2457608 | tf_op jit(solution)/shard_map/ppermute | solution.py:339
  61.4 12.9 %collective-permute-start.7 = (bf16[320,640]{1,0:T(8,128)(2,1)S(1)}, bf16[320,640]{1,0:T(8,128)(2,1)S(1)}, u32[]{:S(2)}, u32[]{:S(2)}) collective-permute-start(bf16[320,640]{1,0:T(8,128)(2,1)S(1)} %get-tuple-element.32), channel_id=1, source_target_pairs={{0,8},{4,12},{8,0},{12,4},{16,24},{20,28},{24,16},{28,20},{1,9},{5... | collective-permute-start | bytes 1228808 | tf_op jit(solution)/shard_map/ppermute | solution.py:325
  64.0 18.7 %collective-permute-start.10 = (bf16[320,640]{1,0:T(8,128)(2,1)S(1)}, bf16[320,640]{1,0:T(8,128)(2,1)S(1)}, u32[]{:S(2)}, u32[]{:S(2)}) collective-permute-start(bf16[320,640]{1,0:T(8,128)(2,1)S(1)} %get-tuple-element.34), channel_id=1, source_target_pairs={{0,8},{4,12},{8,0},{12,4},{16,24},{20,28},{24,16},{28,20},{1,9},{5... | collective-permute-start | bytes 1228808 | tf_op jit(solution)/shard_map/ppermute | solution.py:325
  64.4 29.1 %collective-permute-start.9 = (bf16[512,640]{1,0:T(8,128)(2,1)S(1)}, bf16[512,640]{1,0:T(8,128)(2,1)S(1)}, u32[]{:S(2)}, u32[]{:S(2)}) collective-permute-start(bf16[512,640]{1,0:T(8,128)(2,1)S(1)} %get-tuple-element.33), channel_id=1, source_target_pairs={{0,8},{4,12},{1,9},{5,13},{2,10},{6,14},{3,11},{7,15}} | collective-permute-start | bytes 1966088 | tf_op jit(solution)/shard_map/ppermute | solution.py:325
  68.3 25.3 %collective-permute-start.8 = (bf16[640,640]{1,0:T(8,128)(2,1)S(1)}, bf16[640,640]{1,0:T(8,128)(2,1)S(1)}, u32[]{:S(2)}, u32[]{:S(2)}) collective-permute-start(bf16[640,640]{1,0:T(8,128)(2,1)S(1)} %get-tuple-element.53), channel_id=1, source_target_pairs={{16,8},{20,12},{9,17},{13,21},{18,10},{22,14},{11,19},{15,23}} | collective-permute-start | bytes 2457608 | tf_op jit(solution)/shard_map/ppermute | solution.py:339
  69.3 44.1 %collective-permute-start.4 = (bf16[512,640]{1,0:T(8,128)(2,1)S(1)}, bf16[512,640]{1,0:T(8,128)(2,1)S(1)}, u32[]{:S(2)}, u32[]{:S(2)}) collective-permute-start(bf16[512,640]{1,0:T(8,128)(2,1)S(1)} %constant_dynamic-slice_fusion.6), channel_id=1, source_target_pairs={{0,4},{4,0},{8,12},{12,8},{16,20},{20,16},{24,28},{28,24},{1,5},{5... | collective-permute-start | bytes 1966088 | tf_op jit(solution)/shard_map/ppermute | solution.py:322
  82.9 18.9 %collective-permute-start.11 = (bf16[320,640]{1,0:T(8,128)(2,1)S(1)}, bf16[320,640]{1,0:T(8,128)(2,1)S(1)}, u32[]{:S(2)}, u32[]{:S(2)}) collective-permute-start(bf16[320,640]{1,0:T(8,128)(2,1)S(1)} %get-tuple-element.49), channel_id=1, source_target_pairs={{16,0},{20,4},{8,24},{12,28},{17,1},{21,5},{9,25},{13,29},{18,2},{... | collective-permute-start | bytes 1228808 | tf_op jit(solution)/shard_map/ppermute | solution.py:325
  84.2 17.5 %collective-permute-start.12 = (bf16[320,640]{1,0:T(8,128)(2,1)S(1)}, bf16[320,640]{1,0:T(8,128)(2,1)S(1)}, u32[]{:S(2)}, u32[]{:S(2)}) collective-permute-start(bf16[320,640]{1,0:T(8,128)(2,1)S(1)} %get-tuple-element.59), channel_id=1, source_target_pairs={{16,0},{20,4},{8,24},{12,28},{17,1},{21,5},{9,25},{13,29},{18,2},{... | collective-permute-start | bytes 1228808 | tf_op jit(solution)/shard_map/ppermute | solution.py:325
  102.0 28.7 %collective-permute-start.19 = (bf16[640,640]{1,0:T(8,128)(2,1)S(1)}, bf16[640,640]{1,0:T(8,128)(2,1)S(1)}, u32[]{:S(2)}, u32[]{:S(2)}) collective-permute-start(bf16[640,640]{1,0:T(8,128)(2,1)S(1)} %shard_map.91), channel_id=1, source_target_pairs={{8,16},{12,20},{17,9},{21,13},{10,18},{14,22},{19,11},{23,15}} | collective-permute-start | bytes 2457608 | tf_op jit(solution)/shard_map/ppermute | solution.py:339
  102.7 27.9 %collective-permute-start.18 = (bf16[640,640]{1,0:T(8,128)(2,1)S(1)}, bf16[640,640]{1,0:T(8,128)(2,1)S(1)}, u32[]{:S(2)}, u32[]{:S(2)}) collective-permute-start(bf16[640,640]{1,0:T(8,128)(2,1)S(1)} %shard_map.91), channel_id=1, source_target_pairs={{8,0},{12,4},{17,25},{21,29},{10,2},{14,6},{19,27},{23,31}} | collective-permute-start | bytes 2457608 | tf_op jit(solution)/shard_map/ppermute | solution.py:339
  122.5 14.0 %collective-permute-start.14 = (bf16[320,640]{1,0:T(8,128)(2,1)S(1)}, bf16[320,640]{1,0:T(8,128)(2,1)S(1)}, u32[]{:S(2)}, u32[]{:S(2)}) collective-permute-start(bf16[320,640]{1,0:T(8,128)(2,1)S(1)} %get-tuple-element.66), channel_id=1, source_target_pairs={{0,16},{4,20},{24,8},{28,12},{1,17},{5,21},{25,9},{29,13},{2,18},{... | collective-permute-start | bytes 1228808 | tf_op jit(solution)/shard_map/ppermute | solution.py:325
  128.0 21.1 %collective-permute-start.15 = (bf16[640,640]{1,0:T(8,128)(2,1)S(1)}, bf16[640,640]{1,0:T(8,128)(2,1)S(1)}, u32[]{:S(2)}, u32[]{:S(2)}) collective-permute-start(bf16[640,640]{1,0:T(8,128)(2,1)S(1)} %shard_map.92), channel_id=1, source_target_pairs={{0,8},{4,12},{24,16},{28,20},{1,9},{5,13},{25,17},{29,21},{2,10},{... | collective-permute-start | bytes 2457608 | tf_op jit(solution)/shard_map/ppermute | solution.py:325
  129.4 16.4 %collective-permute-start.16 = (bf16[320,640]{1,0:T(8,128)(2,1)S(1)}, bf16[320,640]{1,0:T(8,128)(2,1)S(1)}, u32[]{:S(2)}, u32[]{:S(2)}) collective-permute-start(bf16[320,640]{1,0:T(8,128)(2,1)S(1)} %collective-permute-done.13), channel_id=1, source_target_pairs={{8,0},{12,4},{16,24},{20,28},{9,1},{13,5},{17,25},{21,29},{10,2},{... | collective-permute-start | bytes 1228808 | tf_op jit(solution)/shard_map/ppermute | solution.py:325
  130.8 18.7 %collective-permute-start.20 = (bf16[640,640]{1,0:T(8,128)(2,1)S(1)}, bf16[640,640]{1,0:T(8,128)(2,1)S(1)}, u32[]{:S(2)}, u32[]{:S(2)}) collective-permute-start(bf16[640,640]{1,0:T(8,128)(2,1)S(1)} %select_select_fusion), channel_id=1, source_target_pairs={{16,24},{20,28},{9,1},{13,5},{18,26},{22,30},{11,3},{15,7}} | collective-permute-start | bytes 2457608 | tf_op jit(solution)/shard_map/ppermute | solution.py:339
  136.5 12.6 %collective-permute-start.17 = (bf16[320,640]{1,0:T(8,128)(2,1)S(1)}, bf16[320,640]{1,0:T(8,128)(2,1)S(1)}, u32[]{:S(2)}, u32[]{:S(2)}) collective-permute-start(bf16[320,640]{1,0:T(8,128)(2,1)S(1)} %collective-permute-done.14), channel_id=1, source_target_pairs={{8,0},{12,4},{16,24},{20,28},{9,1},{13,5},{17,25},{21,29},{10,2},{... | collective-permute-start | bytes 1228808 | tf_op jit(solution)/shard_map/ppermute | solution.py:325
  154.7 13.4 %collective-permute-start.24 = (bf16[512,640]{1,0:T(8,128)(2,1)S(1)}, bf16[512,640]{1,0:T(8,128)(2,1)S(1)}, u32[]{:S(2)}, u32[]{:S(2)}) collective-permute-start(bf16[512,640]{1,0:T(8,128)(2,1)S(1)} %shard_map.95.refs_0_), channel_id=1, source_target_pairs={{0,2},{1,3},{2,0},{3,1},{4,6},{5,7},{6,4},{7,5},{8,10},{9,11},{10,... | collective-permute-start | bytes 1966088 | tf_op jit(solution)/shard_map/ppermute | solution.py:480
  156.2 13.1 %collective-permute-start.21 = (bf16[512,640]{1,0:T(8,128)(2,1)S(1)}, bf16[512,640]{1,0:T(8,128)(2,1)S(1)}, u32[]{:S(2)}, u32[]{:S(2)}) collective-permute-start(bf16[512,640]{1,0:T(8,128)(2,1)S(1)} %shard_map.94), channel_id=1, source_target_pairs={{0,4},{4,0},{8,12},{12,8},{16,20},{20,16},{24,28},{28,24},{1,5},{5... | collective-permute-start | bytes 1966088 | tf_op jit(solution)/shard_map/ppermute | solution.py:322
  157.8 12.4 %collective-permute-start.23 = (bf16[512,640]{1,0:T(8,128)(2,1)S(1)}, bf16[512,640]{1,0:T(8,128)(2,1)S(1)}, u32[]{:S(2)}, u32[]{:S(2)}) collective-permute-start(bf16[512,640]{1,0:T(8,128)(2,1)S(1)} %shard_map.95.refs_0_), channel_id=1, source_target_pairs={{0,1},{1,0},{2,3},{3,2},{4,5},{5,4},{6,7},{7,6},{8,9},{9,8},{10,11... | collective-permute-start | bytes 1966088 | tf_op jit(solution)/shard_map/ppermute | solution.py:480
  169.4 17.1 %collective-permute-start.22 = (bf16[512,640]{1,0:T(8,128)(2,1)S(1)}, bf16[512,640]{1,0:T(8,128)(2,1)S(1)}, u32[]{:S(2)}, u32[]{:S(2)}) collective-permute-start(bf16[512,640]{1,0:T(8,128)(2,1)S(1)} %collective-permute-done.21.refs_4_), channel_id=1, source_target_pairs={{0,2},{1,3},{2,0},{3,1},{4,6},{5,7},{6,4},{7,5},{8,10},{9,11},{10,... | collective-permute-start | bytes 1966088 | tf_op jit(solution)/shard_map/ppermute | solution.py:480
  (24 other events, 197.1 us)
